TPU v7x, 256 devices: a whole 4x4x8 slice. The times are simulated.
256 devices in a mesh: ctx: 8 (over y_lo, x), exp: 32 (over z, y_hi, core).
Axes of the slice: x: 4, y: 4 (y_hi: 2, y_lo: 2; y = y_hi * 2 + y_lo), z: 8, core: 2. Of those that a mesh axis runs over, the one named last changes fastest.
Arguments:
- queries: bfloat16 [2, 256, 64, 576], P(None, 'exp'), may hold values from -512 to 512
- prompt_cache: bfloat16 [32, 4096, 576], P('exp', 'ctx'), may hold values from -6 to 6
- new_latent: bfloat16 [2, 256, 576], P(None, 'exp'), may hold values from -12 to 12
- parents: int32 [32, 8], P('exp'), may hold values from 0 to 7
- lengths: int32 [32], P('exp'), may hold values from 2048 to 4096, as said below
- value_weight: bfloat16 [64, 512, 128], P('exp'), may hold values from -2 to 2
- output_weight: bfloat16 [8192, 7168], P('exp'), may hold values from -0.0625 to 0.0625
- residual: bfloat16 [2, 256, 7168], P(None, 'exp'), may hold values from -6 to 6
- norm_gain: float32 [7168], replicated, may hold values from 0.5 to 1.5
- expert_ids: int32 [2, 256, 8], P(None, 'exp'), may hold values from 0 to 31, all different within a row; in each aligned block of 8 rows (0 to 7, 8 to 15, ..., all dimensions but the last counted through in order) at most 4 rows name the same one
- expert_weights: float32 [2, 256, 8], P(None, 'exp'), may hold values from 0.1 to 1
- expert_gate: bfloat16 [32, 7168, 1024], P('exp', None, 'ctx'), may hold values from -0.0625 to 0.0625
- expert_up: bfloat16 [32, 7168, 1024], P('exp', None, 'ctx'), may hold values from -0.0625 to 0.0625
- expert_down: bfloat16 [32, 1024, 7168], P('exp', 'ctx'), may hold values from -0.1875 to 0.1875
Outputs:
- layer_out: bfloat16 [2, 256, 7168], P(None, 'exp', 'ctx')
Inputs may be any that keep to these rules, and one draw needn't show every extreme that they name: `lengths`: some request uses all 4096 positions. `expert_ids`: each row names 8 different experts; in each aligned block of 8 rows of one step (the rows of one index of exp) no expert is named more than 4 times, a bound that some block reaches.
All inputs are finite; a program needn't handle non-finite values.
Results may differ from a plain program's by a relative error of at most 0.018.
Values may be sent and summed in bfloat16 or wider, within the bound.
A program may use at most 128 MiB of HBM per device.

v0:
```python
import functools

import jax
import jax.numpy as jnp
from jax import lax
from jax.experimental import pallas as pl
from jax.experimental.pallas import tpu as pltpu
from jax.sharding import PartitionSpec as P

SCALE = 0.07216878364870322
NEGATIVE = -1e30
BF16 = jnp.bfloat16
F32 = jnp.float32
N_CTX = 8
N_EXP = 32
ROWS = 16
MINE = 2
HEADS = 64
LAT = 512
COLS = 896
VMEM_LIMIT = 56 * 1024 * 1024


def coordinates():
    c, e = lax.axis_index("ctx"), lax.axis_index("exp")
    x, y_lo = lax.rem(c, 4), c // 4
    z, y_hi, core = e // 4, lax.rem(e // 2, 2), lax.rem(e, 2)
    return c, e, x, y_hi * 2 + y_lo, z, core


def device(x, y, z, core):
    return (lax.rem(y, 2) * 4 + x, z * 4 + (y // 2) * 2 + core)


def greet(barrier, target):
    pl.semaphore_signal(
        barrier, inc=1, device_id=target, device_id_type=pl.DeviceIdType.MESH
    )


def remote(source, target_ref, send_sem, recv_sem, target):
    return pltpu.make_async_remote_copy(
        src_ref=source,
        dst_ref=target_ref,
        send_sem=send_sem,
        recv_sem=recv_sem,
        device_id=target,
        device_id_type=pl.DeviceIdType.MESH,
    )


def one_hot(wanted, columns):
    return jnp.where(
        lax.broadcasted_iota(jnp.int32, (wanted.shape[0], columns), 1) == wanted, 1.0, 0.0
    ).astype(BF16)


def row_index(count):
    return lax.broadcasted_iota(jnp.int32, (count, 1), 0)


def dot(a, b):
    return jnp.dot(a, b, preferred_element_type=F32)


def dot_t(a, b):
    return lax.dot_general(a, b, (((1,), (1,)), ((), ())), preferred_element_type=F32)


def attend_kernel(
    length_ref,
    parents_ref,
    q_ref,
    cache_ref,
    new_ref,
    ids_ref,
    gates_ref,
    out_ref,
    routed_ref,
    part,
    stat,
    got,
    got_stat,
    routes,
    part_send,
    part_recv,
    stat_send,
    stat_recv,
    route_send,
    route_recv,
):
    c, e, x, y, z, core = coordinates()
    barrier = pltpu.get_barrier_semaphore()
    for step in range(1, N_CTX):
        greet(barrier, (lax.rem(c + step, N_CTX), e))

    @pl.loop(1, N_EXP)
    def _(step):
        greet(barrier, (c, lax.rem(e + step, N_EXP)))

    lane = lax.broadcasted_iota(jnp.int32, (ROWS, 128), 1)
    dense = jnp.zeros((ROWS, 128), F32)
    for k in range(8):
        dense = jnp.where(lane == ids_ref[:, k : k + 1], gates_ref[:, k : k + 1], dense)
    spot = core * 16 + (y // 2) * 8 + z
    routes[spot] = dense

    length = length_ref[0]
    positions = cache_ref.shape[0]
    live = (
        c * positions + lax.broadcasted_iota(jnp.int32, (1, positions), 1)
    ) < length
    wide_lane = lax.broadcasted_iota(jnp.int32, (128, 128), 1)

    def partial(target, sums, stats):
        scores = dot_t(q_ref[target], cache_ref[...]) * SCALE
        scores = jnp.where(live, scores, NEGATIVE)
        top = jnp.max(scores, axis=-1, keepdims=True)
        weights = jnp.where(live, jnp.exp(scores - top), 0.0)
        total = jnp.sum(weights, axis=-1, keepdims=True)
        sums[...] = dot(weights.astype(BF16), cache_ref[:, :LAT]).astype(BF16)
        both = jnp.where(wide_lane == 0, top, jnp.where(wide_lane == 1, total, 0.0))
        stats[...] = both.T[:8]

    def copies(target):
        where = (target, e)
        return (
            remote(part.at[target], got.at[c], part_send.at[target], part_recv.at[c], where),
            remote(stat.at[target], got_stat.at[c], stat_send.at[target], stat_recv.at[c], where),
        )

    def route_copy(step):
        target = lax.rem(e + step, N_EXP)
        return remote(
            routes.at[spot],
            routes.at[spot],
            route_send.at[target],
            route_recv.at[spot],
            (c, target),
        )

    first = lax.rem(c + 1, N_CTX)
    partial(first, part.at[first], stat.at[first])
    pl.semaphore_wait(barrier, N_CTX - 1 + N_EXP - 1)
    for copy in copies(first):
        copy.start()

    @pl.loop(2, N_CTX)
    def _(step):
        target = lax.rem(c + step, N_CTX)
        partial(target, part.at[target], stat.at[target])
        for copy in copies(target):
            copy.start()

    @pl.loop(1, N_EXP)
    def _(step):
        route_copy(step).start()

    partial(c, got.at[c], got_stat.at[c])

    row = row_index(128)
    base = lax.rem(c, 4) * MINE
    wanted = jnp.where(
        row == 0,
        c * MINE,
        jnp.where(
            row == 1,
            c * MINE + 1,
            jnp.where(
                row == 2, parents_ref[base], jnp.where(row == 3, parents_ref[base + 1], -1)
            ),
        ),
    )
    keys = dot(one_hot(wanted, ROWS), new_ref[...]).astype(BF16)
    scores = dot_t(q_ref[c], keys) * SCALE
    second = jnp.where(row >= HEADS, 1, 0)
    tail_at = jnp.where(c >= 4, second + 2, -1)
    valid = (wide_lane == second) | (wide_lane == tail_at)
    scores = jnp.where(valid, scores, NEGATIVE)
    top = jnp.max(scores, axis=-1, keepdims=True)
    weights = jnp.where(valid, jnp.exp(scores - top), 0.0)
    own_total = jnp.sum(weights, axis=-1, keepdims=True)
    own_sum = dot(weights.astype(BF16), keys[:, :LAT])

    for step in range(1, N_CTX):
        source = lax.rem(c + N_CTX - step, N_CTX)
        where = (source, e)
        remote(part.at[source], got.at[source], part_send.at[source], part_recv.at[source], where).wait_recv()
        remote(stat.at[source], got_stat.at[source], stat_send.at[source], stat_recv.at[source], where).wait_recv()

    stats = got_stat[...].reshape(N_CTX * 8, 128).T
    peak = top
    for source in range(N_CTX):
        peak = jnp.maximum(peak, stats[:, 8 * source : 8 * source + 1])
    factor = jnp.exp(top - peak)
    total = own_total * factor
    summed = own_sum * factor
    for source in range(N_CTX):
        factor = jnp.exp(stats[:, 8 * source : 8 * source + 1] - peak)
        total = total + stats[:, 8 * source + 1 : 8 * source + 2] * factor
        summed = summed + got[source].astype(F32) * factor
    attended = (summed / total).astype(BF16)
    stacked = jnp.concatenate([attended[:, 128 * k : 128 * k + 128] for k in range(4)], axis=0)
    row = row_index(512)
    source = ((row >> 2) & 3) * 128 + ((row >> 1) & 1) * HEADS + (row >> 4) * 2 + (row & 1)
    out_ref[...] = dot(one_hot(source, 512), stacked).astype(BF16)

    @pl.loop(1, N_EXP)
    def _(step):
        source = lax.rem(e + step, N_EXP)
        at = lax.rem(source, 2) * 16 + lax.rem(source // 2, 2) * 8 + source // 4
        remote(
            routes.at[at], routes.at[at], route_send.at[source], route_recv.at[at], (c, source)
        ).wait_recv()

    everyone = routes[...].reshape(N_EXP * ROWS, 128)
    here = lax.broadcasted_iota(jnp.int32, (N_EXP * ROWS, 128), 1) == e
    weight = jnp.sum(jnp.where(here, everyone, 0.0), axis=-1, keepdims=True)
    routed_ref[...] = jnp.broadcast_to(weight, (N_EXP * ROWS, 128))

    for step in range(1, N_CTX):
        for copy in copies(lax.rem(c + step, N_CTX)):
            copy.wait_send()

    @pl.loop(1, N_EXP)
    def _(step):
        route_copy(step).wait_send()


def project_kernel(
    att_ref,
    wv_ref,
    wo_ref,
    residual_ref,
    gain_ref,
    state_ref,
    normed_ref,
    by_head,
    wo_cols,
    values,
    ordered,
    crossing,
    from_core,
    shares,
    got,
    squares,
    wo_sem,
    head_send,
    head_recv,
    value_send,
    value_recv,
    core_send,
    core_recv,
    share_send,
    share_recv,
    square_send,
    square_recv,
):
    c, e, x, y, z, core = coordinates()
    pair = e // 2
    other_core = (c, e + 1 - 2 * core)
    barrier = pltpu.get_barrier_semaphore()
    for step in range(1, N_CTX):
        greet(barrier, (lax.rem(c + step, N_CTX), e))

    @pl.loop(1, N_EXP)
    def _(step):
        greet(barrier, (c, lax.rem(e + step, N_EXP)))

    columns = pl.ds(pl.multiple_of(c * COLS, 128), COLS)
    fetch = pltpu.make_async_copy(wo_ref.at[:, columns], wo_cols, wo_sem)
    fetch.start()
    by_head[e] = att_ref[e]

    def head_copy(step):
        target = lax.rem(e + step, N_EXP)
        return remote(
            att_ref.at[target], by_head.at[e], head_send.at[target], head_recv.at[e], (c, target)
        )

    pl.semaphore_wait(barrier, N_CTX - 1 + N_EXP - 1)

    @pl.loop(1, N_EXP)
    def _(step):
        head_copy(step).start()

    @pl.loop(1, N_EXP)
    def _(step):
        source = lax.rem(e + step, N_EXP)
        remote(
            att_ref.at[source], by_head.at[source], head_send.at[source], head_recv.at[source], (c, source)
        ).wait_recv()

    row = row_index(512)
    source = (
        ((row >> 1) & 31) * 16 + ((row >> 6) & 3) * 4 + (row & 1) * 2 + (row >> 8)
    )
    latents = dot(one_hot(source, 512), by_head[...].reshape(512, 128)).astype(BF16)
    halves = []
    for parity in range(2):
        total = jnp.zeros((64, 128), F32)
        for quarter in range(4):
            at = (parity * 4 + quarter) * 64
            total = total + dot(
                latents[at : at + 64], wv_ref[parity, 128 * quarter : 128 * quarter + 128, :]
            )
        halves.append(total.astype(BF16))
    values[c] = jnp.concatenate(halves, axis=1)

    def value_copy(target):
        return remote(
            values.at[c], values.at[c], value_send.at[target], value_recv.at[c], (target, e)
        )

    for step in range(1, N_CTX):
        value_copy(lax.rem(c + step, N_CTX)).start()
    for step in range(1, N_CTX):
        source = lax.rem(c + N_CTX - step, N_CTX)
        remote(
            values.at[source], values.at[source], value_send.at[source], value_recv.at[source], (source, e)
        ).wait_recv()
    source = (
        ((row >> 1) & 7) * 64 + ((row >> 4) & 15) * 4 + (row >> 8) * 2 + (row & 1)
    )
    ordered[...] = (
        dot(one_hot(source, 512), values[...].reshape(512, 256)).astype(BF16).reshape(2, 256, 256)
    )
    fetch.wait()
    crossing[...] = dot(ordered[1 - core], wo_cols[...]).astype(BF16).reshape(16, ROWS, COLS)
    across = remote(crossing, from_core, core_send, core_recv, other_core)
    across.start()
    own = dot(ordered[core], wo_cols[...])
    across.wait_recv()
    shares[...] = (
        (own + from_core[...].reshape(256, COLS).astype(F32)).astype(BF16).reshape(16, ROWS, COLS)
    )

    def share_copy(step):
        target = lax.rem(pair + step, 16)
        return remote(
            shares.at[target],
            got.at[pair],
            share_send.at[target],
            share_recv.at[pair],
            (c, target * 2 + core),
        )

    @pl.loop(1, 16)
    def _(step):
        share_copy(step).start()

    got[pair] = shares[pair]

    @pl.loop(1, 16)
    def _(step):
        source = lax.rem(pair + step, 16)
        remote(
            shares.at[source],
            got.at[source],
            share_send.at[source],
            share_recv.at[source],
            (c, source * 2 + core),
        ).wait_recv()

    state = residual_ref[:, columns].astype(F32)
    state = state + jnp.sum(got[...].astype(F32), axis=0)
    state_ref[...] = state
    square = jnp.sum(state * state, axis=-1, keepdims=True)
    squares[c] = jnp.broadcast_to(square, (ROWS, 128))

    def square_copy(target):
        return remote(
            squares.at[c], squares.at[c], square_send.at[target], square_recv.at[c], (target, e)
        )

    for step in range(1, N_CTX):
        square_copy(lax.rem(c + step, N_CTX)).start()
    for step in range(1, N_CTX):
        source = lax.rem(c + N_CTX - step, N_CTX)
        remote(
            squares.at[source], squares.at[source], square_send.at[source], square_recv.at[source], (source, e)
        ).wait_recv()
    mean = jnp.sum(squares[...], axis=0)[:, :1] * (1.0 / (N_CTX * COLS))
    normed_ref[...] = (state * lax.rsqrt(mean + 1e-06) * gain_ref[pl.ds(c, 1), :]).astype(BF16)

    across.wait_send()
    for step in range(1, N_CTX):
        value_copy(lax.rem(c + step, N_CTX)).wait_send()
        square_copy(lax.rem(c + step, N_CTX)).wait_send()

    @pl.loop(1, N_EXP)
    def _(step):
        head_copy(step).wait_send()

    @pl.loop(1, 16)
    def _(step):
        share_copy(step).wait_send()


def expert_kernel(
    normed_ref,
    state_ref,
    routed_ref,
    gate_ref,
    up_ref,
    down_ref,
    out_ref,
    rows,
    sums,
    from_core,
    half_one,
    whole_one,
    half_two,
    whole_two,
    last,
    hidden,
    both,
    down,
    weight_sems,
    z_send,
    z_recv,
    two_send,
    two_recv,
    relay_two_send,
    relay_two_recv,
    three_send,
    three_recv,
    relay_three_send,
    relay_three_recv,
    share_send,
    share_recv,
    cross_send,
    cross_recv,
    half_one_send,
    half_one_recv,
    whole_one_send,
    whole_one_recv,
    half_two_send,
    half_two_recv,
    whole_two_send,
    whole_two_recv,
    last_send,
    last_recv,
):
    c, e, x, y, z, core = coordinates()
    y_hi = y // 2

    def plus(a, k):
        return lax.rem(a + k, 4)

    neighbours = {
        ("x", 0): device(plus(x, 1), y, z, core),
        ("x", 1): device(plus(x, 3), y, z, core),
        ("y", 0): device(x, plus(y, 1), z, core),
        ("y", 1): device(x, plus(y, 3), z, core),
    }
    other_core = device(x, y, z, 1 - core)
    wide_axis, narrow_axis = ("x", "y"), ("y", "x")
    wide_at, narrow_at = (x, y), (y, x)

    barrier = pltpu.get_barrier_semaphore()
    for target in neighbours.values():
        greet(barrier, target)
    greet(barrier, other_core)
    for step in range(1, 8):
        greet(barrier, device(x, y, lax.rem(z + step, 8), core))

    fetches = [
        pltpu.make_async_copy(gate_ref, both.at[:, :, pl.ds(0, 128)], weight_sems.at[0]),
        pltpu.make_async_copy(up_ref, both.at[:, :, pl.ds(128, 128)], weight_sems.at[1]),
        pltpu.make_async_copy(down_ref, down, weight_sems.at[2]),
    ]
    for fetch in fetches:
        fetch.start()
    rows[c, core, y_hi, z] = normed_ref[...]
    pl.semaphore_wait(barrier, 12)

    sent = []

    def send(source, target_ref, send_sem, recv_sem, target):
        copy = remote(source, target_ref, send_sem, recv_sem, target)
        copy.start()
        sent.append(copy)

    def arrive(ref, send_sem, recv_sem, target):
        remote(ref, ref, send_sem, recv_sem, target).wait_recv()

    def chunk(ref, part, wide, narrow, start=0, count=4):
        at_x, at_y = (wide, narrow) if part == 0 else (narrow, wide)
        return ref.at[
            lax.rem(at_y, 2) * 4 + at_x, core, at_y // 2, pl.ds(part * 4 + start, count)
        ]

    for step in range(1, 8):
        to = lax.rem(z + step, 8)
        block = rows.at[c, core, y_hi, z]
        send(block, block, z_send.at[to], z_recv.at[z], device(x, y, to, core))
    for step in range(1, 8):
        source = lax.rem(z + step, 8)
        arrive(
            rows.at[c, core, y_hi, source],
            z_send.at[source],
            z_recv.at[source],
            device(x, y, source, core),
        )

    def share(part, wide, narrow):
        block = chunk(rows, part, wide, narrow)
        sem = (part, wide, narrow)
        send(block, block, share_send.at[sem], share_recv.at[sem], other_core)

    def spread(part, narrow):
        block = chunk(rows, part, wide_at[part], narrow)
        for side in range(2):
            sem = (part, side, narrow)
            send(
                block,
                block,
                three_send.at[sem],
                three_recv.at[sem],
                neighbours[wide_axis[part], side],
            )
        share(part, wide_at[part], narrow)

    for part in range(2):
        block = chunk(rows, part, wide_at[part], narrow_at[part])
        for side in range(2):
            send(
                block,
                block,
                two_send.at[part, side],
                two_recv.at[part, side],
                neighbours[narrow_axis[part], side],
            )
    for part in range(2):
        spread(part, narrow_at[part])
    for part in range(2):
        for side in range(2):
            near = plus(narrow_at[part], 3 if side == 0 else 1)
            target = neighbours[narrow_axis[part], side]
            arrive(
                chunk(rows, part, wide_at[part], near),
                two_send.at[part, side],
                two_recv.at[part, side],
                target,
            )
            block = chunk(rows, part, wide_at[part], near, 2 * side, 2)
            send(
                block,
                block,
                relay_two_send.at[part, side],
                relay_two_recv.at[part, side],
                target,
            )
            spread(part, near)
    for part in range(2):
        far = plus(narrow_at[part], 2)
        for side in range(2):
            arrive(
                chunk(rows, part, wide_at[part], far, 2 * side, 2),
                relay_two_send.at[part, side],
                relay_two_recv.at[part, side],
                neighbours[narrow_axis[part], side],
            )
        spread(part, far)
    for step in range(4):
        for part in range(2):
            narrow = plus(narrow_at[part], (0, 1, 3, 2)[step])
            for side in range(2):
                near = plus(wide_at[part], 3 if side == 0 else 1)
                target = neighbours[wide_axis[part], side]
                sem = (part, side, narrow)
                arrive(
                    chunk(rows, part, near, narrow), three_send.at[sem], three_recv.at[sem], target
                )
                share(part, near, narrow)

                @pl.when((narrow >= 2) == (side == 1))
                def _():
                    block = chunk(rows, part, near, narrow)
                    remote(
                        block,
                        block,
                        relay_three_send.at[part, narrow],
                        relay_three_recv.at[part, narrow],
                        target,
                    ).start()

    for part in range(2):
        for narrow in range(4):
            side = narrow // 2
            far = plus(wide_at[part], 2)
            arrive(
                chunk(rows, part, far, narrow),
                relay_three_send.at[part, narrow],
                relay_three_recv.at[part, narrow],
                neighbours[wide_axis[part], side],
            )
            share(part, far, narrow)
    for part in range(2):
        for wide in range(4):
            for narrow in range(4):
                at_x, at_y = (wide, narrow) if part == 0 else (narrow, wide)
                sem = (part, wide, narrow)
                block = rows.at[
                    (at_y % 2) * 4 + at_x, 1 - core, at_y // 2, pl.ds(part * 4, 4)
                ]
                arrive(block, share_send.at[sem], share_recv.at[sem], other_core)

    for fetch in fetches:
        fetch.wait()
    total = jnp.zeros((512, 256), F32)
    for k in range(N_CTX):
        total = total + dot(rows[k].reshape(512, COLS), both[k])
    gate, up = total[:, :128], total[:, 128:]
    silu = gate / (1.0 + jnp.exp(-gate))
    hidden[...] = (silu * up * routed_ref[...]).astype(BF16).reshape(2, 256, 128)

    for k in range(N_CTX):
        at = pl.ds(k * COLS, COLS)
        sums[k, 1 - core] = (
            dot(hidden[1 - core], down[:, at]).astype(BF16).reshape(2, 8, ROWS, COLS)
        )
        send(
            sums.at[k, 1 - core], from_core.at[k], cross_send.at[k], cross_recv.at[k], other_core
        )
    for k in range(N_CTX):
        at = pl.ds(k * COLS, COLS)
        own = dot(hidden[core], down[:, at])
        arrive(from_core.at[k], cross_send.at[k], cross_recv.at[k], other_core)
        sums[k, core] = (
            (own + from_core[k].reshape(256, COLS).astype(F32))
            .astype(BF16)
            .reshape(2, 8, ROWS, COLS)
        )

    def add(ref, *others):
        value = ref[...].astype(F32)
        for other in others:
            value = value + other[...].astype(F32)
        ref[...] = value.astype(BF16)

    def wide_send(part, side, narrow):
        near = plus(wide_at[part], 1 if side == 0 else 3)
        sem = (part, side, narrow)
        send(
            chunk(sums, part, near, narrow),
            whole_one.at[sem],
            whole_one_send.at[sem],
            whole_one_recv.at[sem],
            neighbours[wide_axis[part], side],
        )

    for part in range(2):
        far = plus(wide_at[part], 2)
        for side in range(2):
            for k in range(2):
                sem = (part, side, k)
                send(
                    chunk(sums, part, far, 2 * side + k),
                    half_one.at[sem],
                    half_one_send.at[sem],
                    half_one_recv.at[sem],
                    neighbours[wide_axis[part], side],
                )
    for part in range(2):
        for side in range(2):
            for k in range(2):
                wide_send(part, side, 2 * (1 - side) + k)
    for part in range(2):
        for side in range(2):
            near = plus(wide_at[part], 1 if side == 0 else 3)
            for k in range(2):
                sem = (part, side, k)
                arrive(
                    half_one.at[sem],
                    half_one_send.at[sem],
                    half_one_recv.at[sem],
                    neighbours[wide_axis[part], side],
                )
                add(chunk(sums, part, near, 2 * side + k), half_one.at[sem])
                wide_send(part, side, 2 * side + k)

    def narrow_send(part, side):
        near = plus(narrow_at[part], 1 if side == 0 else 3)
        sem = (part, side)
        send(
            chunk(sums, part, wide_at[part], near),
            whole_two.at[sem],
            whole_two_send.at[sem],
            whole_two_recv.at[sem],
            neighbours[narrow_axis[part], side],
        )

    for step in (2, 1, 3, 0):
        for part in range(2):
            narrow = plus(narrow_at[part], step)
            for side in range(2):
                sem = (part, side, narrow)
                arrive(
                    whole_one.at[sem],
                    whole_one_send.at[sem],
                    whole_one_recv.at[sem],
                    neighbours[wide_axis[part], side],
                )
            add(
                chunk(sums, part, wide_at[part], narrow),
                whole_one.at[part, 0, narrow],
                whole_one.at[part, 1, narrow],
            )
            if step == 2:
                for side in range(2):
                    sem = (part, side)
                    send(
                        chunk(sums, part, wide_at[part], narrow, 2 * side, 2),
                        half_two.at[sem],
                        half_two_send.at[sem],
                        half_two_recv.at[sem],
                        neighbours[narrow_axis[part], side],
                    )
    for part in range(2):
        for side in range(2):
            near = plus(narrow_at[part], 1 if side == 0 else 3)
            sem = (part, side)
            arrive(
                half_two.at[sem],
                half_two_send.at[sem],
                half_two_recv.at[sem],
                neighbours[narrow_axis[part], side],
            )
            add(chunk(sums, part, wide_at[part], near, 2 * side, 2), half_two.at[sem])
            narrow_send(part, side)
    for part in range(2):
        for side in range(2):
            sem = (part, side)
            arrive(
                whole_two.at[sem],
                whole_two_send.at[sem],
                whole_two_recv.at[sem],
                neighbours[narrow_axis[part], side],
            )
        add(
            chunk(sums, part, wide_at[part], narrow_at[part]),
            whole_two.at[part, 0],
            whole_two.at[part, 1],
        )
    for step in range(1, 8):
        to = lax.rem(z + step, 8)
        send(
            sums.at[c, core, y_hi, to],
            last.at[z],
            last_send.at[to],
            last_recv.at[z],
            device(x, y, to, core),
        )
    last[z] = sums[c, core, y_hi, z]
    for step in range(1, 8):
        source = lax.rem(z + step, 8)
        arrive(
            last.at[source],
            last_send.at[source],
            last_recv.at[source],
            device(x, y, source, core),
        )
    result = state_ref[...]
    for k in range(8):
        result = result + last[k].astype(F32)
    out_ref[...] = result.astype(BF16)

    for copy in sent:
        copy.wait_send()
    for part in range(2):
        for narrow in range(4):
            block = chunk(rows, part, wide_at[part], narrow)
            remote(
                block,
                block,
                relay_three_send.at[part, narrow],
                relay_three_recv.at[part, narrow],
                neighbours[wide_axis[part], narrow // 2],
            ).wait_send()


VMEM = pl.BlockSpec(memory_space=pltpu.VMEM)
SMEM = pl.BlockSpec(memory_space=pltpu.SMEM)
ANY = pl.BlockSpec(memory_space=pl.ANY)
DMA = pltpu.SemaphoreType.DMA


def params(number):
    return pltpu.CompilerParams(
        collective_id=number, has_side_effects=True, vmem_limit_bytes=VMEM_LIMIT
    )


def per_device(
    queries,
    prompt_cache,
    new_latent,
    parents,
    lengths,
    value_weight,
    output_weight,
    residual,
    norm_gain,
    expert_ids,
    expert_weights,
    expert_gate,
    expert_up,
    expert_down,
):
    key_width = queries.shape[3]
    attended, routed = pl.pallas_call(
        attend_kernel,
        out_shape=(
            jax.ShapeDtypeStruct((512, 128), BF16),
            jax.ShapeDtypeStruct((N_EXP * ROWS, 128), F32),
        ),
        in_specs=[SMEM, SMEM] + [VMEM] * 5,
        out_specs=(VMEM, VMEM),
        scratch_shapes=[
            pltpu.VMEM((N_CTX, 128, LAT), BF16),
            pltpu.VMEM((N_CTX, 8, 128), F32),
            pltpu.VMEM((N_CTX, 128, LAT), BF16),
            pltpu.VMEM((N_CTX, 8, 128), F32),
            pltpu.VMEM((N_EXP, ROWS, 128), F32),
            DMA((N_CTX,)),
            DMA((N_CTX,)),
            DMA((N_CTX,)),
            DMA((N_CTX,)),
            DMA((N_EXP,)),
            DMA((N_EXP,)),
        ],
        compiler_params=params(0),
        name="attend",
    )(
        lengths,
        parents.reshape(8),
        queries.reshape(N_CTX, 128, key_width),
        prompt_cache[0],
        new_latent.reshape(ROWS, key_width),
        expert_ids.reshape(ROWS, 8),
        expert_weights.reshape(ROWS, 8),
    )
    state, normed = pl.pallas_call(
        project_kernel,
        out_shape=(
            jax.ShapeDtypeStruct((ROWS, COLS), F32),
            jax.ShapeDtypeStruct((ROWS, COLS), BF16),
        ),
        in_specs=[VMEM, VMEM, ANY, VMEM, VMEM],
        out_specs=(VMEM, VMEM),
        scratch_shapes=[
            pltpu.VMEM((N_EXP, ROWS, 128), BF16),
            pltpu.VMEM((256, COLS), BF16),
            pltpu.VMEM((N_CTX, 64, 256), BF16),
            pltpu.VMEM((2, 256, 256), BF16),
            pltpu.VMEM((16, ROWS, COLS), BF16),
            pltpu.VMEM((16, ROWS, COLS), BF16),
            pltpu.VMEM((16, ROWS, COLS), BF16),
            pltpu.VMEM((16, ROWS, COLS), BF16),
            pltpu.VMEM((N_CTX, ROWS, 128), F32),
            DMA,
            DMA((N_EXP,)),
            DMA((N_EXP,)),
            DMA((N_CTX,)),
            DMA((N_CTX,)),
            DMA,
            DMA,
            DMA((16,)),
            DMA((16,)),
            DMA((N_CTX,)),
            DMA((N_CTX,)),
        ],
        compiler_params=params(1),
        name="project",
    )(
        attended.reshape(N_EXP, ROWS, 128),
        value_weight,
        output_weight,
        residual.reshape(ROWS, N_CTX * COLS),
        norm_gain.reshape(N_CTX, COLS),
    )
    out = pl.pallas_call(
        expert_kernel,
        out_shape=jax.ShapeDtypeStruct((ROWS, COLS), BF16),
        in_specs=[VMEM, VMEM, VMEM, ANY, ANY, ANY],
        out_specs=VMEM,
        scratch_shapes=[
            pltpu.VMEM((N_CTX, 2, 2, 8, ROWS, COLS), BF16),
            pltpu.VMEM((N_CTX, 2, 2, 8, ROWS, COLS), BF16),
            pltpu.VMEM((N_CTX, 2, 8, ROWS, COLS), BF16),
            pltpu.VMEM((2, 2, 2, 4, ROWS, COLS), BF16),
            pltpu.VMEM((2, 2, 4, 4, ROWS, COLS), BF16),
            pltpu.VMEM((2, 2, 2, ROWS, COLS), BF16),
            pltpu.VMEM((2, 2, 4, ROWS, COLS), BF16),
            pltpu.VMEM((8, ROWS, COLS), BF16),
            pltpu.VMEM((2, 256, 128), BF16),
            pltpu.VMEM((N_CTX, COLS, 256), BF16),
            pltpu.VMEM((128, N_CTX * COLS), BF16),
            DMA((3,)),
            DMA((8,)),
            DMA((8,)),
            DMA((2, 2)),
            DMA((2, 2)),
            DMA((2, 2)),
            DMA((2, 2)),
            DMA((2, 2, 4)),
            DMA((2, 2, 4)),
            DMA((2, 4)),
            DMA((2, 4)),
            DMA((2, 4, 4)),
            DMA((2, 4, 4)),
            DMA((8,)),
            DMA((8,)),
            DMA((2, 2, 2)),
            DMA((2, 2, 2)),
            DMA((2, 2, 4)),
            DMA((2, 2, 4)),
            DMA((2, 2)),
            DMA((2, 2)),
            DMA((2, 2)),
            DMA((2, 2)),
            DMA((8,)),
            DMA((8,)),
        ],
        compiler_params=params(2),
        name="experts",
    )(
        normed,
        state,
        routed,
        expert_gate.reshape(N_CTX, COLS, 128),
        expert_up.reshape(N_CTX, COLS, 128),
        expert_down[0],
    )
    return out.reshape(2, 8, COLS)


def solution(mesh):
    in_specs = (
        P(None, "exp", None, None),
        P("exp", "ctx", None),
        P(None, "exp", None),
        P("exp", None),
        P("exp"),
        P("exp", None, None),
        P("exp", None),
        P(None, "exp", None),
        P(),
        P(None, "exp", None),
        P(None, "exp", None),
        P("exp", None, "ctx"),
        P("exp", None, "ctx"),
        P("exp", "ctx", None),
    )
    out_specs = P(None, "exp", "ctx")
    return jax.shard_map(
        per_device, mesh=mesh, in_specs=in_specs, out_specs=out_specs, check_vma=False
    )
```

profile of v0, /device:TPU:1, one launch (start us, length us, event | category | flops | bytes accessed | tf_op | source)
XLA Modules:
  0.0 160.6 jit_solution(10048589633676282853)
XLA Ops:
  0.0 0.0 copy-start
  0.0 2.2 %copy.15 = bf16[1,512,576]{2,1,0:T(8,128)(2,1)} copy(bf16[1,512,576]{1,2,0:T(8,128)(2,1)} %param.15) | data formatting | bytes 1179648 | tf_op args[1]
  2.8 35.8 %attend.1 = (bf16[512,128]{1,0:T(8,128)(2,1)}, f32[512,128]{1,0:T(8,128)}) custom-call(s32[1]{0:T(128)S(6)} %copy.23.length_ref, s32[8]{0:T(128)} %bitcast.23, bf16[8,128,576]{2,1,0:T(8,128)(2,1)} %bitcast.16, bf16[512,576]{1,0:T(8,128)(2,1)} %bitcast.12, bf16[16,576]{1,0:T(8,128)(2,1)} %bitcast.20, s32[16,8]{1,0:T(8,128)} %bitcast.21, f32[16,8]{1,0:T(8,128)} %bitcast.22), custom_call_target="tpu_custom_call" | custom-call | tf_op jit(solution)/shard_map/attend/pallas_call | solution.py:813
  38.6 0.0 copy-done
  38.7 0.6 reshape.40.gain_ref
  39.3 39.9 %project.1 = (f32[16,896]{1,0:T(8,128)}, bf16[16,896]{1,0:T(8,128)(2,1)}) custom-call(bf16[32,16,128]{2,1,0:T(8,128)(2,1)} %bitcast.18, bf16[2,512,128]{2,1,0:T(8,128)(2,1)} %wv_ref.1, bf16[256,7168]{1,0:T(8,128)(2,1)} %wo_ref.1, bf16[16,7168]{1,0:T(8,128)(2,1)} %bitcast.17, f32[8,896]{1,0:T(8,128)} %reshape.40.gain_ref), custom_call_target="tpu_custom_call" | custom-call | tf_op jit(solution)/shard_map/project/pallas_call | solution.py:845
  79.1 80.1 %experts.1 = bf16[16,896]{1,0:T(8,128)(2,1)} custom-call(bf16[16,896]{1,0:T(8,128)(2,1)} %get-tuple-element.10.normed_ref, f32[16,896]{1,0:T(8,128)} %get-tuple-element.11.state_ref, f32[512,128]{1,0:T(8,128)} %get-tuple-element.12.routed_ref, bf16[8,896,128]{2,1,0:T(8,128)(2,1)} %bitcast.13, bf16[8,896,128]{2,1,0:T(8,128)(2,1)} %bitcast.14, ...), custom_call_target="tpu_custom_call" | custom-call | tf_op jit(solution)/shard_map/experts/pallas_call | solution.py:884
  159.2 1.4 copy.24
Async XLA Ops:
  0.0 38.6 %copy-start = (f32[7168]{0:T(1024)S(1)}, f32[7168]{0:T(1024)}, u32[]{:S(2)}) copy-start(f32[7168]{0:T(1024)} %param.22) | copy-start | bytes 86020
where the time goes:
time: 163 us; the launch traced here: 161 us
  Pallas kernels  156 us (96%)
  local copies, waits for them, and re-layouts  4.13 us (3%)
    pallas_call x1, Pallas kernels, per_device(): pl.pallas_call(expert_kernel, out_shape=jax.ShapeDtypeStruct((ROWS, COLS)...  80.1 us
    pallas_call x1, Pallas kernels, per_device(): pl.pallas_call(project_kernel, out_shape=(jax.ShapeDtypeStruct((ROWS, COL...  39.9 us
    pallas_call x1, Pallas kernels, per_device(): pl.pallas_call(attend_kernel, out_shape=(jax.ShapeDtypeStruct((512, 128),...  35.8 us
    unnamed x4, local copies, waits for them, and re-layouts  3.51 us

commit v1 on v0

v1 whole, which is shorter than its diff:
```python
import functools

import jax
import jax.numpy as jnp
from jax import lax
from jax.experimental import pallas as pl
from jax.experimental.pallas import tpu as pltpu
from jax.sharding import PartitionSpec as P

SCALE = 0.07216878364870322
NEGATIVE = -1e30
BF16 = jnp.bfloat16
F32 = jnp.float32
N_CTX = 8
N_EXP = 32
ROWS = 16
MINE = 2
HEADS = 64
LAT = 512
COLS = 896
VMEM_LIMIT = 56 * 1024 * 1024


def coordinates():
    c, e = lax.axis_index("ctx"), lax.axis_index("exp")
    x, y_lo = lax.rem(c, 4), c // 4
    z, y_hi, core = e // 4, lax.rem(e // 2, 2), lax.rem(e, 2)
    return c, e, x, y_hi * 2 + y_lo, z, core


def device(x, y, z, core):
    return (lax.rem(y, 2) * 4 + x, z * 4 + (y // 2) * 2 + core)


def greet(barrier, target):
    pl.semaphore_signal(
        barrier, inc=1, device_id=target, device_id_type=pl.DeviceIdType.MESH
    )


def remote(source, target_ref, send_sem, recv_sem, target):
    return pltpu.make_async_remote_copy(
        src_ref=source,
        dst_ref=target_ref,
        send_sem=send_sem,
        recv_sem=recv_sem,
        device_id=target,
        device_id_type=pl.DeviceIdType.MESH,
    )


def one_hot(wanted, columns):
    return jnp.where(
        lax.broadcasted_iota(jnp.int32, (wanted.shape[0], columns), 1) == wanted, 1.0, 0.0
    ).astype(BF16)


def row_index(count):
    return lax.broadcasted_iota(jnp.int32, (count, 1), 0)


def dot(a, b):
    return jnp.dot(a, b, preferred_element_type=F32)


def dot_t(a, b):
    return lax.dot_general(a, b, (((1,), (1,)), ((), ())), preferred_element_type=F32)


def layer_kernel(
    length_ref,
    parents_ref,
    q_ref,
    cache_ref,
    new_ref,
    ids_ref,
    gates_ref,
    wv_ref,
    wo_ref,
    residual_ref,
    gain_ref,
    gate_ref,
    up_ref,
    down_ref,
    out_ref,
    part,
    stat,
    got,
    got_stat,
    orders,
    heads,
    by_head,
    wo_cols,
    values,
    ordered,
    crossing,
    crossed,
    shares,
    from_y,
    from_z,
    squares,
    state,
    notes,
    noted,
    rows,
    sums,
    from_core,
    half_one,
    whole_one,
    half_two,
    whole_two,
    last,
    hidden,
    both,
    down,
    weight_sems,
    part_send,
    part_recv,
    stat_send,
    stat_recv,
    head_send,
    head_recv,
    value_send,
    value_recv,
    crossing_send,
    crossing_recv,
    y_send,
    y_recv,
    zsum_send,
    zsum_recv,
    square_send,
    square_recv,
    note_send,
    note_recv,
    z_send,
    z_recv,
    two_send,
    two_recv,
    relay_two_send,
    relay_two_recv,
    three_send,
    three_recv,
    relay_three_send,
    relay_three_recv,
    share_send,
    share_recv,
    cross_send,
    cross_recv,
    half_one_send,
    half_one_recv,
    whole_one_send,
    whole_one_recv,
    half_two_send,
    half_two_recv,
    whole_two_send,
    whole_two_recv,
    last_send,
    last_recv,
):
    c, e, x, y, z, core = coordinates()
    y_hi, y_lo = y // 2, lax.rem(y, 2)

    def plus(a, k):
        return lax.rem(a + k, 4)

    neighbours = {
        ("x", 0): device(plus(x, 1), y, z, core),
        ("x", 1): device(plus(x, 3), y, z, core),
        ("y", 0): device(x, plus(y, 1), z, core),
        ("y", 1): device(x, plus(y, 3), z, core),
    }
    other_core = device(x, y, z, 1 - core)
    wide_axis, narrow_axis = ("x", "y"), ("y", "x")
    wide_at, narrow_at = (x, y), (y, x)

    barrier = pltpu.get_barrier_semaphore()
    for step in range(1, N_CTX):
        greet(barrier, (lax.rem(c + step, N_CTX), e))

    @pl.loop(1, N_EXP)
    def _(step):
        greet(barrier, (c, lax.rem(e + step, N_EXP)))

    greet(barrier, device(x, 3 - y, z, core))

    columns = pl.ds(pl.multiple_of(c * COLS, 128), COLS)
    fetches = [
        pltpu.make_async_copy(wo_ref.at[:, columns], wo_cols, weight_sems.at[0]),
        pltpu.make_async_copy(gate_ref, both.at[:, :, pl.ds(0, 128)], weight_sems.at[1]),
        pltpu.make_async_copy(up_ref, both.at[:, :, pl.ds(128, 128)], weight_sems.at[2]),
        pltpu.make_async_copy(down_ref, down, weight_sems.at[3]),
    ]
    for fetch in fetches:
        fetch.start()

    sent = []

    def send(source, target_ref, send_sem, recv_sem, target):
        copy = remote(source, target_ref, send_sem, recv_sem, target)
        copy.start()
        sent.append(copy)

    def arrive(ref, send_sem, recv_sem, target):
        remote(ref, ref, send_sem, recv_sem, target).wait_recv()

    length = length_ref[0]
    positions = cache_ref.shape[1]
    live = (
        c * positions + lax.broadcasted_iota(jnp.int32, (1, positions), 1)
    ) < length
    wide_lane = lax.broadcasted_iota(jnp.int32, (128, 128), 1)

    def partial(target, sums_ref, stats_ref):
        scores = dot(q_ref[target], cache_ref[...]) * SCALE
        scores = jnp.where(live, scores, NEGATIVE)
        top = jnp.max(scores, axis=-1, keepdims=True)
        weights = jnp.where(live, jnp.exp(scores - top), 0.0)
        total = jnp.sum(weights, axis=-1, keepdims=True)
        sums_ref[...] = dot_t(weights.astype(BF16), cache_ref[:LAT, :]).astype(BF16)
        stats_ref[...] = jnp.where(
            wide_lane == 0, top, jnp.where(wide_lane == 1, total, 0.0)
        ).T[:8]

    def peer(flip, step):
        return lax.rem(y_lo + flip, 2) * 4 + plus(x, step)

    def send_partial(target):
        where = (target, e)
        send(part.at[target], got.at[c], part_send.at[target], part_recv.at[c], where)
        send(stat.at[target], got_stat.at[c], stat_send.at[target], stat_recv.at[c], where)

    peers = [peer(*k) for k in ((1, 2), (0, 2), (1, 1), (0, 1), (1, 3), (0, 3), (1, 0))]
    partial(peers[0], part.at[peers[0]], stat.at[peers[0]])
    pl.semaphore_wait(barrier, N_CTX - 1 + N_EXP - 1 + 1)
    send_partial(peers[0])
    for target in peers[1:]:
        partial(target, part.at[target], stat.at[target])
        send_partial(target)
    partial(c, got.at[c], got_stat.at[c])

    row = row_index(512)
    orders[0] = one_hot(
        ((row >> 2) & 3) * 128 + ((row >> 1) & 1) * HEADS + (row >> 4) * 2 + (row & 1), 512
    )
    orders[1] = one_hot(
        ((row >> 1) & 31) * 16 + ((row >> 6) & 3) * 4 + (row & 1) * 2 + (row >> 8), 512
    )
    orders[2] = one_hot(
        ((row >> 1) & 7) * 64
        + ((row >> 4) & 7) * 8
        + ((row >> 7) & 1) * 4
        + (row >> 8) * 2
        + (row & 1),
        512,
    )

    row = row_index(128)
    base = lax.rem(c, 4) * MINE
    wanted = jnp.where(
        row == 0,
        c * MINE,
        jnp.where(
            row == 1,
            c * MINE + 1,
            jnp.where(
                row == 2, parents_ref[base], jnp.where(row == 3, parents_ref[base + 1], -1)
            ),
        ),
    )
    keys = dot(one_hot(wanted, ROWS), new_ref[...]).astype(BF16)
    scores = dot_t(q_ref[c], keys) * SCALE
    second = jnp.where(row >= HEADS, 1, 0)
    tail_at = jnp.where(c >= 4, second + 2, -1)
    valid = (wide_lane == second) | (wide_lane == tail_at)
    scores = jnp.where(valid, scores, NEGATIVE)
    top = jnp.max(scores, axis=-1, keepdims=True)
    weights = jnp.where(valid, jnp.exp(scores - top), 0.0)
    own_total = jnp.sum(weights, axis=-1, keepdims=True)
    own_sum = dot(weights.astype(BF16), keys[:, :LAT])

    lane = lax.broadcasted_iota(jnp.int32, (ROWS, 128), 1)
    dense = jnp.zeros((ROWS, 128), F32)
    for k in range(8):
        dense = jnp.where(lane == ids_ref[:, k : k + 1], gates_ref[:, k : k + 1], dense)

    for source in peers:
        where = (source, e)
        arrive(got_stat.at[source], stat_send.at[source], stat_recv.at[source], where)
    stats = got_stat[...].reshape(N_CTX * 8, 128).T
    peak = top
    for source in range(N_CTX):
        peak = jnp.maximum(peak, stats[:, 8 * source : 8 * source + 1])
    factor = jnp.exp(top - peak)
    total = own_total * factor
    summed = own_sum * factor
    for source in range(N_CTX):
        factor = jnp.exp(stats[:, 8 * source : 8 * source + 1] - peak)
        total = total + stats[:, 8 * source + 1 : 8 * source + 2] * factor
    for source in peers:
        arrive(got.at[source], part_send.at[source], part_recv.at[source], (source, e))
    for source in range(N_CTX):
        factor = jnp.exp(stats[:, 8 * source : 8 * source + 1] - peak)
        summed = summed + got[source].astype(F32) * factor
    attended = (summed / total).astype(BF16)
    stacked = jnp.concatenate([attended[:, 128 * k : 128 * k + 128] for k in range(4)], axis=0)
    heads[...] = dot(orders[0], stacked).astype(BF16).reshape(N_EXP, ROWS, 128)

    def head_copy(step):
        target = lax.rem(e + step, N_EXP)
        return remote(
            heads.at[target], by_head.at[e], head_send.at[target], head_recv.at[e], (c, target)
        )

    @pl.loop(1, N_EXP)
    def _(step):
        head_copy(step).start()

    by_head[e] = heads[e]

    @pl.loop(1, N_EXP)
    def _(step):
        source = lax.rem(e + step, N_EXP)
        remote(
            heads.at[source],
            by_head.at[source],
            head_send.at[source],
            head_recv.at[source],
            (c, source),
        ).wait_recv()

    latents = dot(orders[1], by_head[...].reshape(512, 128)).astype(BF16)
    halves = []
    for parity in range(2):
        value = jnp.zeros((64, 128), F32)
        for quarter in range(4):
            at = (parity * 4 + quarter) * 64
            value = value + dot(
                latents[at : at + 64], wv_ref[parity, 128 * quarter : 128 * quarter + 128, :]
            )
        halves.append(value.astype(BF16))
    values[c] = jnp.concatenate(halves, axis=1)

    for target in peers:
        send(values.at[c], values.at[c], value_send.at[target], value_recv.at[c], (target, e))
    for source in peers:
        arrive(values.at[source], value_send.at[source], value_recv.at[source], (source, e))
    ordered[...] = dot(orders[2], values[...].reshape(512, 256)).astype(BF16).reshape(2, 256, 256)
    fetches[0].wait()
    crossing[...] = dot(ordered[1 - core], wo_cols[...]).astype(BF16).reshape(2, 8, ROWS, COLS)
    for half in (1, 0):
        at = lax.rem(y_hi + half, 2)
        send(
            crossing.at[at],
            crossed.at[at],
            crossing_send.at[at],
            crossing_recv.at[at],
            other_core,
        )
    other_y = device(x, plus(y, 2), z, core)
    for half in (1, 0):
        at = lax.rem(y_hi + half, 2)
        own = dot(ordered[core, pl.ds(pl.multiple_of(at * 128, 128), 128)], wo_cols[...])
        arrive(crossed.at[at], crossing_send.at[at], crossing_recv.at[at], other_core)
        own = own + crossed[at].reshape(128, COLS).astype(F32)
        shares[at] = own.astype(BF16).reshape(8, ROWS, COLS)
        if half:
            for step in (4, 3, 5, 2, 6, 1, 7, 0):
                to = lax.rem(z + step, 8)
                send(shares.at[at, to], from_y.at[to], y_send.at[to], y_recv.at[to], other_y)
    for step in (4, 3, 5, 2, 6, 1, 7, 0):
        to = lax.rem(z + step, 8)
        arrive(from_y.at[to], y_send.at[to], y_recv.at[to], other_y)
        both_y = shares[y_hi, to].astype(F32) + from_y[to].astype(F32)
        if step:
            shares[y_hi, to] = both_y.astype(BF16)
            send(
                shares.at[y_hi, to],
                from_z.at[z],
                zsum_send.at[to],
                zsum_recv.at[z],
                device(x, y, to, core),
            )
    value = residual_ref[:, columns].astype(F32) + both_y
    for step in range(1, 8):
        source = lax.rem(z + step, 8)
        arrive(
            from_z.at[source],
            zsum_send.at[source],
            zsum_recv.at[source],
            device(x, y, source, core),
        )
        value = value + from_z[source].astype(F32)
    state[...] = value
    rows[c, core, y_hi, z] = (value * gain_ref[pl.ds(c, 1), :]).astype(BF16)
    squares[c] = jnp.broadcast_to(jnp.sum(value * value, axis=-1, keepdims=True), (ROWS, 128))
    for target in peers:
        send(squares.at[c], squares.at[c], square_send.at[target], square_recv.at[c], (target, e))

    def note_copy(step):
        target = lax.rem(e + step, N_EXP)
        spot = core * 16 + y_hi * 8 + z
        return remote(
            notes.at[target], noted.at[spot], note_send.at[target], note_recv.at[spot], (c, target)
        )

    def send_notes():
        for source in peers:
            arrive(squares.at[source], square_send.at[source], square_recv.at[source], (source, e))
        mean = jnp.sum(squares[...], axis=0) * (1.0 / (N_CTX * COLS))
        scale = lax.rsqrt(mean + 1e-06)
        block = jnp.concatenate([dense, scale, jnp.zeros((96, 128), F32)], axis=0).T
        notes[...] = block[:N_EXP].reshape(N_EXP, 1, 128)
        noted[core * 16 + y_hi * 8 + z] = notes[e]

        @pl.loop(1, N_EXP)
        def _(step):
            note_copy(step).start()

    def chunk(ref, part, wide, narrow, start=0, count=4):
        at_x, at_y = (wide, narrow) if part == 0 else (narrow, wide)
        return ref.at[
            lax.rem(at_y, 2) * 4 + at_x, core, at_y // 2, pl.ds(part * 4 + start, count)
        ]

    for step in range(1, 8):
        to = lax.rem(z + step, 8)
        block = rows.at[c, core, y_hi, z]
        send(block, block, z_send.at[to], z_recv.at[z], device(x, y, to, core))
    for step in range(1, 8):
        source = lax.rem(z + step, 8)
        arrive(
            rows.at[c, core, y_hi, source],
            z_send.at[source],
            z_recv.at[source],
            device(x, y, source, core),
        )

    def share(part, wide, narrow):
        block = chunk(rows, part, wide, narrow)
        sem = (part, wide, narrow)
        send(block, block, share_send.at[sem], share_recv.at[sem], other_core)

    def spread(part, narrow):
        block = chunk(rows, part, wide_at[part], narrow)
        for side in range(2):
            sem = (part, side, narrow)
            send(
                block,
                block,
                three_send.at[sem],
                three_recv.at[sem],
                neighbours[wide_axis[part], side],
            )
        share(part, wide_at[part], narrow)

    for part in range(2):
        block = chunk(rows, part, wide_at[part], narrow_at[part])
        for side in range(2):
            send(
                block,
                block,
                two_send.at[part, side],
                two_recv.at[part, side],
                neighbours[narrow_axis[part], side],
            )
    for part in range(2):
        spread(part, narrow_at[part])
    send_notes()
    for part in range(2):
        for side in range(2):
            near = plus(narrow_at[part], 3 if side == 0 else 1)
            target = neighbours[narrow_axis[part], side]
            arrive(
                chunk(rows, part, wide_at[part], near),
                two_send.at[part, side],
                two_recv.at[part, side],
                target,
            )
            block = chunk(rows, part, wide_at[part], near, 2 * side, 2)
            send(
                block,
                block,
                relay_two_send.at[part, side],
                relay_two_recv.at[part, side],
                target,
            )
            spread(part, near)
    for part in range(2):
        far = plus(narrow_at[part], 2)
        for side in range(2):
            arrive(
                chunk(rows, part, wide_at[part], far, 2 * side, 2),
                relay_two_send.at[part, side],
                relay_two_recv.at[part, side],
                neighbours[narrow_axis[part], side],
            )
        spread(part, far)
    for step in range(4):
        for part in range(2):
            narrow = plus(narrow_at[part], (0, 1, 3, 2)[step])
            for side in range(2):
                near = plus(wide_at[part], 3 if side == 0 else 1)
                target = neighbours[wide_axis[part], side]
                sem = (part, side, narrow)
                arrive(
                    chunk(rows, part, near, narrow), three_send.at[sem], three_recv.at[sem], target
                )
                share(part, near, narrow)

                @pl.when((narrow >= 2) == (side == 1))
                def _():
                    block = chunk(rows, part, near, narrow)
                    remote(
                        block,
                        block,
                        relay_three_send.at[part, narrow],
                        relay_three_recv.at[part, narrow],
                        target,
                    ).start()

    for part in range(2):
        for narrow in range(4):
            side = narrow // 2
            far = plus(wide_at[part], 2)
            arrive(
                chunk(rows, part, far, narrow),
                relay_three_send.at[part, narrow],
                relay_three_recv.at[part, narrow],
                neighbours[wide_axis[part], side],
            )
            share(part, far, narrow)
    for part in range(2):
        for wide in range(4):
            for narrow in range(4):
                at_x, at_y = (wide, narrow) if part == 0 else (narrow, wide)
                sem = (part, wide, narrow)
                block = rows.at[
                    (at_y % 2) * 4 + at_x, 1 - core, at_y // 2, pl.ds(part * 4, 4)
                ]
                arrive(block, share_send.at[sem], share_recv.at[sem], other_core)

    for fetch in fetches[1:]:
        fetch.wait()

    @pl.loop(1, N_EXP)
    def _(step):
        source = lax.rem(e + step, N_EXP)
        spot = lax.rem(source, 2) * 16 + lax.rem(source // 2, 2) * 8 + source // 4
        remote(
            notes.at[source], noted.at[spot], note_send.at[source], note_recv.at[spot], (c, source)
        ).wait_recv()

    note = jnp.broadcast_to(noted[...], (N_EXP, ROWS, 128)).reshape(N_EXP * ROWS, 128)
    lane = lax.broadcasted_iota(jnp.int32, (N_EXP * ROWS, 128), 1)
    beam = row_index(N_EXP * ROWS) & 15
    routed = jnp.sum(jnp.where(lane == beam, note, 0.0), axis=-1, keepdims=True)
    scale = jnp.sum(jnp.where(lane == beam + 16, note, 0.0), axis=-1, keepdims=True)
    total = jnp.zeros((512, 256), F32)
    for k in range(N_CTX):
        total = total + dot(rows[k].reshape(512, COLS), both[k])
    total = total * scale
    gate, up = total[:, :128], total[:, 128:]
    silu = gate / (1.0 + jnp.exp(-gate))
    hidden[...] = (silu * up * routed).astype(BF16).reshape(2, 256, 128)

    def far_send(part):
        far = plus(wide_at[part], 2)
        for side in range(2):
            for k in range(2):
                sem = (part, side, k)
                send(
                    chunk(sums, part, far, 2 * side + k),
                    half_one.at[sem],
                    half_one_send.at[sem],
                    half_one_recv.at[sem],
                    neighbours[wide_axis[part], side],
                )

    blocks = [
        peer(*k) for k in ((0, 2), (1, 2), (0, 1), (0, 3), (0, 0), (1, 1), (1, 3), (1, 0))
    ]
    for k in blocks:
        at = pl.ds(pl.multiple_of(k * COLS, 128), COLS)
        sums[k, 1 - core] = (
            dot(hidden[1 - core], down[:, at]).astype(BF16).reshape(2, 8, ROWS, COLS)
        )
        send(
            sums.at[k, 1 - core], from_core.at[k], cross_send.at[k], cross_recv.at[k], other_core
        )
    for number, k in enumerate(blocks):
        at = pl.ds(pl.multiple_of(k * COLS, 128), COLS)
        own = dot(hidden[core], down[:, at])
        arrive(from_core.at[k], cross_send.at[k], cross_recv.at[k], other_core)
        sums[k, core] = (
            (own + from_core[k].reshape(256, COLS).astype(F32))
            .astype(BF16)
            .reshape(2, 8, ROWS, COLS)
        )
        if number == 1:
            far_send(0)
        if number == 4:
            far_send(1)

    def add(ref, *others):
        value = ref[...].astype(F32)
        for other in others:
            value = value + other[...].astype(F32)
        ref[...] = value.astype(BF16)

    def wide_send(part, side, narrow):
        near = plus(wide_at[part], 1 if side == 0 else 3)
        sem = (part, side, narrow)
        send(
            chunk(sums, part, near, narrow),
            whole_one.at[sem],
            whole_one_send.at[sem],
            whole_one_recv.at[sem],
            neighbours[wide_axis[part], side],
        )

    for part in range(2):
        for side in range(2):
            for k in range(2):
                wide_send(part, side, 2 * (1 - side) + k)
    for part in range(2):
        for side in range(2):
            near = plus(wide_at[part], 1 if side == 0 else 3)
            for k in range(2):
                sem = (part, side, k)
                arrive(
                    half_one.at[sem],
                    half_one_send.at[sem],
                    half_one_recv.at[sem],
                    neighbours[wide_axis[part], side],
                )
                add(chunk(sums, part, near, 2 * side + k), half_one.at[sem])
                wide_send(part, side, 2 * side + k)

    def narrow_send(part, side):
        near = plus(narrow_at[part], 1 if side == 0 else 3)
        sem = (part, side)
        send(
            chunk(sums, part, wide_at[part], near),
            whole_two.at[sem],
            whole_two_send.at[sem],
            whole_two_recv.at[sem],
            neighbours[narrow_axis[part], side],
        )

    for step in (2, 1, 3, 0):
        for part in range(2):
            narrow = plus(narrow_at[part], step)
            for side in range(2):
                sem = (part, side, narrow)
                arrive(
                    whole_one.at[sem],
                    whole_one_send.at[sem],
                    whole_one_recv.at[sem],
                    neighbours[wide_axis[part], side],
                )
            add(
                chunk(sums, part, wide_at[part], narrow),
                whole_one.at[part, 0, narrow],
                whole_one.at[part, 1, narrow],
            )
            if step == 2:
                for side in range(2):
                    sem = (part, side)
                    send(
                        chunk(sums, part, wide_at[part], narrow, 2 * side, 2),
                        half_two.at[sem],
                        half_two_send.at[sem],
                        half_two_recv.at[sem],
                        neighbours[narrow_axis[part], side],
                    )
    for part in range(2):
        for side in range(2):
            near = plus(narrow_at[part], 1 if side == 0 else 3)
            sem = (part, side)
            arrive(
                half_two.at[sem],
                half_two_send.at[sem],
                half_two_recv.at[sem],
                neighbours[narrow_axis[part], side],
            )
            add(chunk(sums, part, wide_at[part], near, 2 * side, 2), half_two.at[sem])
            narrow_send(part, side)
    for part in range(2):
        for side in range(2):
            sem = (part, side)
            arrive(
                whole_two.at[sem],
                whole_two_send.at[sem],
                whole_two_recv.at[sem],
                neighbours[narrow_axis[part], side],
            )
        add(
            chunk(sums, part, wide_at[part], narrow_at[part]),
            whole_two.at[part, 0],
            whole_two.at[part, 1],
        )
    for step in range(1, 8):
        to = lax.rem(z + step, 8)
        send(
            sums.at[c, core, y_hi, to],
            last.at[z],
            last_send.at[to],
            last_recv.at[z],
            device(x, y, to, core),
        )
    last[z] = sums[c, core, y_hi, z]
    for step in range(1, 8):
        source = lax.rem(z + step, 8)
        arrive(
            last.at[source],
            last_send.at[source],
            last_recv.at[source],
            device(x, y, source, core),
        )
    result = state[...]
    for k in range(8):
        result = result + last[k].astype(F32)
    out_ref[...] = result.astype(BF16)

    for copy in sent:
        copy.wait_send()
    for part in range(2):
        for narrow in range(4):
            block = chunk(rows, part, wide_at[part], narrow)
            remote(
                block,
                block,
                relay_three_send.at[part, narrow],
                relay_three_recv.at[part, narrow],
                neighbours[wide_axis[part], narrow // 2],
            ).wait_send()

    @pl.loop(1, N_EXP)
    def _(step):
        head_copy(step).wait_send()
        note_copy(step).wait_send()


VMEM = pl.BlockSpec(memory_space=pltpu.VMEM)
SMEM = pl.BlockSpec(memory_space=pltpu.SMEM)
ANY = pl.BlockSpec(memory_space=pl.ANY)
DMA = pltpu.SemaphoreType.DMA


def per_device(
    queries,
    prompt_cache,
    new_latent,
    parents,
    lengths,
    value_weight,
    output_weight,
    residual,
    norm_gain,
    expert_ids,
    expert_weights,
    expert_gate,
    expert_up,
    expert_down,
):
    key_width = queries.shape[3]
    pairs = [(N_CTX,), (N_CTX,), (N_EXP,), (N_CTX,), (2,), (8,), (8,), (N_CTX,), (N_EXP,)]
    pairs += [(8,), (2, 2), (2, 2), (2, 2, 4), (2, 4), (2, 4, 4)]
    pairs += [(8,), (2, 2, 2), (2, 2, 4), (2, 2), (2, 2), (8,)]
    out = pl.pallas_call(
        layer_kernel,
        out_shape=jax.ShapeDtypeStruct((ROWS, COLS), BF16),
        in_specs=[SMEM, SMEM] + [VMEM] * 6 + [ANY, VMEM, VMEM, ANY, ANY, ANY],
        out_specs=VMEM,
        scratch_shapes=[
            pltpu.VMEM((N_CTX, 128, LAT), BF16),
            pltpu.VMEM((N_CTX, 8, 128), F32),
            pltpu.VMEM((N_CTX, 128, LAT), BF16),
            pltpu.VMEM((N_CTX, 8, 128), F32),
            pltpu.VMEM((3, 512, 512), BF16),
            pltpu.VMEM((N_EXP, ROWS, 128), BF16),
            pltpu.VMEM((N_EXP, ROWS, 128), BF16),
            pltpu.VMEM((256, COLS), BF16),
            pltpu.VMEM((N_CTX, 64, 256), BF16),
            pltpu.VMEM((2, 256, 256), BF16),
            pltpu.VMEM((2, 8, ROWS, COLS), BF16),
            pltpu.VMEM((2, 8, ROWS, COLS), BF16),
            pltpu.VMEM((2, 8, ROWS, COLS), BF16),
            pltpu.VMEM((8, ROWS, COLS), BF16),
            pltpu.VMEM((8, ROWS, COLS), BF16),
            pltpu.VMEM((N_CTX, ROWS, 128), F32),
            pltpu.VMEM((ROWS, COLS), F32),
            pltpu.VMEM((N_EXP, 1, 128), F32),
            pltpu.VMEM((N_EXP, 1, 128), F32),
            pltpu.VMEM((N_CTX, 2, 2, 8, ROWS, COLS), BF16),
            pltpu.VMEM((N_CTX, 2, 2, 8, ROWS, COLS), BF16),
            pltpu.VMEM((N_CTX, 2, 8, ROWS, COLS), BF16),
            pltpu.VMEM((2, 2, 2, 4, ROWS, COLS), BF16),
            pltpu.VMEM((2, 2, 4, 4, ROWS, COLS), BF16),
            pltpu.VMEM((2, 2, 2, ROWS, COLS), BF16),
            pltpu.VMEM((2, 2, 4, ROWS, COLS), BF16),
            pltpu.VMEM((8, ROWS, COLS), BF16),
            pltpu.VMEM((2, 256, 128), BF16),
            pltpu.VMEM((N_CTX, COLS, 256), BF16),
            pltpu.VMEM((128, N_CTX * COLS), BF16),
            DMA((4,)),
        ]
        + [DMA(shape) for shape in pairs for _ in range(2)],
        compiler_params=pltpu.CompilerParams(
            collective_id=0, has_side_effects=True, vmem_limit_bytes=VMEM_LIMIT
        ),
        name="layer",
    )(
        lengths,
        parents.reshape(8),
        queries.reshape(N_CTX, 128, key_width),
        prompt_cache[0].T,
        new_latent.reshape(ROWS, key_width),
        expert_ids.reshape(ROWS, 8),
        expert_weights.reshape(ROWS, 8),
        value_weight,
        output_weight,
        residual.reshape(ROWS, N_CTX * COLS),
        norm_gain.reshape(N_CTX, COLS),
        expert_gate.reshape(N_CTX, COLS, 128),
        expert_up.reshape(N_CTX, COLS, 128),
        expert_down[0],
    )
    return out.reshape(2, 8, COLS)


def solution(mesh):
    in_specs = (
        P(None, "exp", None, None),
        P("exp", "ctx", None),
        P(None, "exp", None),
        P("exp", None),
        P("exp"),
        P("exp", None, None),
        P("exp", None),
        P(None, "exp", None),
        P(),
        P(None, "exp", None),
        P(None, "exp", None),
        P("exp", None, "ctx"),
        P("exp", None, "ctx"),
        P("exp", "ctx", None),
    )
    out_specs = P(None, "exp", "ctx")
    return jax.shard_map(
        per_device, mesh=mesh, in_specs=in_specs, out_specs=out_specs, check_vma=False
    )
```

time: 163 us -> 140 us (0.86); the launches traced: 161 us -> 140 us
  Pallas kernels: 156 us -> 136 us
    pallas_call x3 -> x1, Pallas kernels: 156 us -> 136 us  [per_device(): pl.pallas_call(layer_kernel, out_shape=jax.ShapeDtypeStruct((ROWS, COLS),...]
    unnamed x4 -> x1, local copies, waits for them, and re-layouts: 3.51 us -> 1.36 us
where the time goes in v1:
time: 140 us
  Pallas kernels  136 us (97%)
  local copies, waits for them, and re-layouts  2.72 us (2%)
    pallas_call x1, Pallas kernels, per_device(): pl.pallas_call(layer_kernel, out_shape=jax.ShapeDtypeStruct((ROWS, COLS),...  136 us

profile of v1, /device:TPU:1, one launch (start us, length us, event | category | flops | bytes accessed | tf_op | source)
XLA Modules:
  0.0 139.7 jit_solution(5981818283725291399)
XLA Ops:
  0.7 1.4 reshape.36.gain_ref
  2.0 136.3 %layer.1 = bf16[16,896]{1,0:T(8,128)(2,1)} custom-call(s32[1]{0:T(128)S(6)} %copy.22.length_ref, s32[8]{0:T(128)} %bitcast.23, bf16[8,128,576]{2,1,0:T(8,128)(2,1)} %bitcast.16, bf16[576,512]{1,0:T(8,128)(2,1)} %bitcast.17, bf16[16,576]{1,0:T(8,128)(2,1)} %bitcast.20, s32[16,8]{1,0:T(8,128)} %bitcast.21, f32[16,8]{1,0:T(8,128)} %bitcast.22, ...), custom_call_target="tpu_custom_call" | custom-call | tf_op jit(solution)/shard_map/layer/pallas_call | solution.py:770
  138.3 1.4 copy.23

commit v2 on v1

--- a/solution.py
+++ b/solution.py
@@ -18,6 +18,8 @@
 HEADS = 64
 LAT = 512
 COLS = 896
+PARTS = ((0, 384), (384, 256), (640, 256))
+HALVES = ((2, 1), (3, 0))
 VMEM_LIMIT = 56 * 1024 * 1024
 
 
@@ -109,6 +111,9 @@
     whole_one,
     half_two,
     whole_two,
+    ring_sums,
+    y_sums,
+    x_sums,
     last,
     hidden,
     both,
@@ -134,6 +139,10 @@
     note_recv,
     z_send,
     z_recv,
+    x_send,
+    x_recv,
+    y_row_send,
+    y_row_recv,
     two_send,
     two_recv,
     relay_two_send,
@@ -142,8 +151,12 @@
     three_recv,
     relay_three_send,
     relay_three_recv,
+    ring_send,
+    ring_recv,
     share_send,
     share_recv,
+    share_z_send,
+    share_z_recv,
     cross_send,
     cross_recv,
     half_one_send,
@@ -154,6 +167,12 @@
     half_two_recv,
     whole_two_send,
     whole_two_recv,
+    ring_sum_send,
+    ring_sum_recv,
+    y_sum_send,
+    y_sum_recv,
+    x_sum_send,
+    x_sum_recv,
     last_send,
     last_recv,
 ):
@@ -416,34 +435,50 @@
         def _(step):
             note_copy(step).start()
 
-    def chunk(ref, part, wide, narrow, start=0, count=4):
+    def chunk(ref, part, wide, narrow, start=0, count=8):
         at_x, at_y = (wide, narrow) if part == 0 else (narrow, wide)
+        first_lane, lanes = PARTS[part]
         return ref.at[
-            lax.rem(at_y, 2) * 4 + at_x, core, at_y // 2, pl.ds(part * 4 + start, count)
+            lax.rem(at_y, 2) * 4 + at_x,
+            core,
+            at_y // 2,
+            pl.ds(start, count),
+            :,
+            pl.ds(first_lane, lanes),
         ]
 
-    for step in range(1, 8):
+    def layer(ref, at_z, at_y):
+        return ref.at[pl.ds(lax.rem(at_y, 2) * 4, 4), core, at_y // 2, at_z, :, pl.ds(*PARTS[2])]
+
+    along_z = (device(x, y, lax.rem(z + 1, 8), core), device(x, y, lax.rem(z + 7, 8), core))
+
+    def behind(side, hop):
+        return lax.rem(z + (8 - hop if side == 0 else hop), 8)
+
+    for step in (4, 3, 5, 2, 6, 1, 7):
         to = lax.rem(z + step, 8)
-        block = rows.at[c, core, y_hi, z]
+        block = rows.at[c, core, y_hi, z, :, pl.ds(0, PARTS[2][0])]
         send(block, block, z_send.at[to], z_recv.at[z], device(x, y, to, core))
-    for step in range(1, 8):
-        source = lax.rem(z + step, 8)
-        arrive(
-            rows.at[c, core, y_hi, source],
-            z_send.at[source],
-            z_recv.at[source],
-            device(x, y, source, core),
-        )
-
-    def share(part, wide, narrow):
+    block = rows.at[c, core, y_hi, z, :, pl.ds(*PARTS[2])]
+    for step in (2, 1, 3):
+        send(
+            block,
+            block,
+            x_send.at[step],
+            x_recv.at[step],
+            device(plus(x, step), y, z, core),
+        )
+
+    def share(part, wide, narrow, step, hop):
         block = chunk(rows, part, wide, narrow)
-        sem = (part, wide, narrow)
+        sem = (part, step, hop)
         send(block, block, share_send.at[sem], share_recv.at[sem], other_core)
 
-    def spread(part, narrow):
+    def spread(part, step):
+        narrow = plus(narrow_at[part], step)
         block = chunk(rows, part, wide_at[part], narrow)
         for side in range(2):
-            sem = (part, side, narrow)
+            sem = (part, side, step)
             send(
                 block,
                 block,
@@ -451,8 +486,44 @@
                 three_recv.at[sem],
                 neighbours[wide_axis[part], side],
             )
-        share(part, wide_at[part], narrow)
-
+        share(part, wide_at[part], narrow, step, 0)
+
+    def spread_z(step):
+        block = layer(rows, z, plus(y, step))
+        for side in range(2):
+            sem = (side, 0, step)
+            send(block, block, ring_send.at[sem], ring_recv.at[sem], along_z[side])
+
+    def share_z(at_z, hop):
+        block = rows.at[:, core, :, at_z, :, pl.ds(*PARTS[2])]
+        send(block, block, share_z_send.at[hop], share_z_recv.at[hop], other_core)
+
+    for step in (1, 3, 2):
+        source = plus(x, 4 - step)
+        arrive(
+            rows.at[y_lo * 4 + source, core, y_hi, z, :, pl.ds(*PARTS[2])],
+            x_send.at[step],
+            x_recv.at[step],
+            device(source, y, z, core),
+        )
+    block = layer(rows, z, y)
+    for step in (2, 1, 3):
+        send(
+            block,
+            block,
+            y_row_send.at[step],
+            y_row_recv.at[step],
+            device(x, plus(y, step), z, core),
+        )
+    spread_z(0)
+    for step in range(1, 8):
+        source = lax.rem(z + step, 8)
+        arrive(
+            rows.at[c, core, y_hi, source, :, pl.ds(0, PARTS[2][0])],
+            z_send.at[source],
+            z_recv.at[source],
+            device(x, y, source, core),
+        )
     for part in range(2):
         block = chunk(rows, part, wide_at[part], narrow_at[part])
         for side in range(2):
@@ -464,11 +535,21 @@
                 neighbours[narrow_axis[part], side],
             )
     for part in range(2):
-        spread(part, narrow_at[part])
-    send_notes()
+        spread(part, 0)
+    for step in (1, 3, 2):
+        source = plus(y, 4 - step)
+        arrive(
+            layer(rows, z, source),
+            y_row_send.at[step],
+            y_row_recv.at[step],
+            device(x, source, z, core),
+        )
+        spread_z(4 - step)
+    share_z(z, 0)
     for part in range(2):
         for side in range(2):
-            near = plus(narrow_at[part], 3 if side == 0 else 1)
+            step = 3 if side == 0 else 1
+            near = plus(narrow_at[part], step)
             target = neighbours[narrow_axis[part], side]
             arrive(
                 chunk(rows, part, wide_at[part], near),
@@ -476,7 +557,7 @@
                 two_recv.at[part, side],
                 target,
             )
-            block = chunk(rows, part, wide_at[part], near, 2 * side, 2)
+            block = chunk(rows, part, wide_at[part], near, 4 * side, 4)
             send(
                 block,
                 block,
@@ -484,59 +565,98 @@
                 relay_two_recv.at[part, side],
                 target,
             )
-            spread(part, near)
+            spread(part, step)
+    send_notes()
+
+    def ring(hop):
+        for step in (0, 3, 1, 2):
+            for side in range(2):
+                if hop == 4 and (step in (0, 3)) != (side == 0):
+                    continue
+                block = layer(rows, behind(side, hop), plus(y, step))
+                sem = (side, hop - 1, step)
+                arrive(block, ring_send.at[sem], ring_recv.at[sem], along_z[side])
+                if hop < 3 or (hop == 3 and (step in (0, 3)) == (side == 0)):
+                    sem = (side, hop, step)
+                    send(block, block, ring_send.at[sem], ring_recv.at[sem], along_z[side])
+        if hop < 4:
+            for side in range(2):
+                share_z(behind(side, hop), 2 * hop - 1 + side)
+        else:
+            share_z(behind(0, 4), 7)
+
+    def near(step):
+        for part in range(2):
+            narrow = plus(narrow_at[part], step)
+            for side in range(2):
+                wide = plus(wide_at[part], 3 if side == 0 else 1)
+                target = neighbours[wide_axis[part], side]
+                sem = (part, side, step)
+                block = chunk(rows, part, wide, narrow)
+                arrive(block, three_send.at[sem], three_recv.at[sem], target)
+                if (step in (0, 3)) == (side == 0):
+                    send(
+                        block,
+                        block,
+                        relay_three_send.at[part, step],
+                        relay_three_recv.at[part, step],
+                        target,
+                    )
+                share(part, wide, narrow, step, 1 + side)
+
+    near(0)
+    ring(1)
     for part in range(2):
         far = plus(narrow_at[part], 2)
         for side in range(2):
             arrive(
-                chunk(rows, part, wide_at[part], far, 2 * side, 2),
+                chunk(rows, part, wide_at[part], far, 4 * side, 4),
                 relay_two_send.at[part, side],
                 relay_two_recv.at[part, side],
                 neighbours[narrow_axis[part], side],
             )
-        spread(part, far)
-    for step in range(4):
+        spread(part, 2)
+    near(3)
+    near(1)
+    ring(2)
+    near(2)
+    ring(3)
+    ring(4)
+    for step in (0, 3, 1, 2):
         for part in range(2):
-            narrow = plus(narrow_at[part], (0, 1, 3, 2)[step])
-            for side in range(2):
-                near = plus(wide_at[part], 3 if side == 0 else 1)
-                target = neighbours[wide_axis[part], side]
-                sem = (part, side, narrow)
-                arrive(
-                    chunk(rows, part, near, narrow), three_send.at[sem], three_recv.at[sem], target
-                )
-                share(part, near, narrow)
-
-                @pl.when((narrow >= 2) == (side == 1))
-                def _():
-                    block = chunk(rows, part, near, narrow)
-                    remote(
-                        block,
-                        block,
-                        relay_three_send.at[part, narrow],
-                        relay_three_recv.at[part, narrow],
-                        target,
-                    ).start()
-
+            side = 0 if step in (0, 3) else 1
+            wide, narrow = plus(wide_at[part], 2), plus(narrow_at[part], step)
+            arrive(
+                chunk(rows, part, wide, narrow),
+                relay_three_send.at[part, step],
+                relay_three_recv.at[part, step],
+                neighbours[wide_axis[part], side],
+            )
+            share(part, wide, narrow, step, 3)
+    for hop in range(8):
+        source = z if hop == 0 else behind(0, 4) if hop == 7 else behind((hop - 1) % 2, (hop + 1) // 2)
+        arrive(
+            rows.at[:, 1 - core, :, source, :, pl.ds(*PARTS[2])],
+            share_z_send.at[hop],
+            share_z_recv.at[hop],
+            other_core,
+        )
     for part in range(2):
-        for narrow in range(4):
-            side = narrow // 2
-            far = plus(wide_at[part], 2)
-            arrive(
-                chunk(rows, part, far, narrow),
-                relay_three_send.at[part, narrow],
-                relay_three_recv.at[part, narrow],
-                neighbours[wide_axis[part], side],
-            )
-            share(part, far, narrow)
-    for part in range(2):
-        for wide in range(4):
-            for narrow in range(4):
+        first_lane, lanes = PARTS[part]
+        for step in range(4):
+            for hop in range(4):
+                wide = plus(wide_at[part], (0, 3, 1, 2)[hop])
+                narrow = plus(narrow_at[part], step)
                 at_x, at_y = (wide, narrow) if part == 0 else (narrow, wide)
-                sem = (part, wide, narrow)
                 block = rows.at[
-                    (at_y % 2) * 4 + at_x, 1 - core, at_y // 2, pl.ds(part * 4, 4)
+                    lax.rem(at_y, 2) * 4 + at_x,
+                    1 - core,
+                    at_y // 2,
+                    :,
+                    :,
+                    pl.ds(first_lane, lanes),
                 ]
+                sem = (part, step, hop)
                 arrive(block, share_send.at[sem], share_recv.at[sem], other_core)
 
     for fetch in fetches[1:]:
@@ -563,177 +683,295 @@
     silu = gate / (1.0 + jnp.exp(-gate))
     hidden[...] = (silu * up * routed).astype(BF16).reshape(2, 256, 128)
 
-    def far_send(part):
-        far = plus(wide_at[part], 2)
-        for side in range(2):
-            for k in range(2):
-                sem = (part, side, k)
-                send(
-                    chunk(sums, part, far, 2 * side + k),
-                    half_one.at[sem],
-                    half_one_send.at[sem],
-                    half_one_recv.at[sem],
-                    neighbours[wide_axis[part], side],
-                )
-
-    blocks = [
-        peer(*k) for k in ((0, 2), (1, 2), (0, 1), (0, 3), (0, 0), (1, 1), (1, 3), (1, 0))
-    ]
-    for k in blocks:
-        at = pl.ds(pl.multiple_of(k * COLS, 128), COLS)
-        sums[k, 1 - core] = (
-            dot(hidden[1 - core], down[:, at]).astype(BF16).reshape(2, 8, ROWS, COLS)
-        )
-        send(
-            sums.at[k, 1 - core], from_core.at[k], cross_send.at[k], cross_recv.at[k], other_core
-        )
-    for number, k in enumerate(blocks):
-        at = pl.ds(pl.multiple_of(k * COLS, 128), COLS)
-        own = dot(hidden[core], down[:, at])
-        arrive(from_core.at[k], cross_send.at[k], cross_recv.at[k], other_core)
-        sums[k, core] = (
-            (own + from_core[k].reshape(256, COLS).astype(F32))
-            .astype(BF16)
-            .reshape(2, 8, ROWS, COLS)
-        )
-        if number == 1:
-            far_send(0)
-        if number == 4:
-            far_send(1)
-
     def add(ref, *others):
         value = ref[...].astype(F32)
         for other in others:
             value = value + other[...].astype(F32)
         ref[...] = value.astype(BF16)
 
-    def wide_send(part, side, narrow):
-        near = plus(wide_at[part], 1 if side == 0 else 3)
-        sem = (part, side, narrow)
-        send(
-            chunk(sums, part, near, narrow),
-            whole_one.at[sem],
-            whole_one_send.at[sem],
-            whole_one_recv.at[sem],
-            neighbours[wide_axis[part], side],
-        )
-
-    for part in range(2):
+    def landed(ref, part, *index):
+        return ref.at[(part, *index, slice(None), slice(None), pl.ds(0, PARTS[part][1]))]
+
+    def piece(ref, part):
+        return ref.at[:, :, :, pl.ds(*PARTS[part])]
+
+    blocks = [
+        peer(*k) for k in ((0, 2), (1, 2), (0, 1), (0, 3), (0, 0), (1, 1), (1, 3), (1, 0))
+    ]
+
+    def product(part, k, half):
+        first_lane, lanes = PARTS[part]
+        at = pl.ds(pl.multiple_of(k * COLS + first_lane, 128), lanes)
+        return dot(hidden[half], down[:, at])
+
+    def other(part):
+        for k in blocks:
+            block = piece(sums.at[k, 1 - core], part)
+            block[...] = (
+                product(part, k, 1 - core).astype(BF16).reshape(2, 8, ROWS, PARTS[part][1])
+            )
+            send(
+                block,
+                piece(from_core.at[k], part),
+                cross_send.at[part, k],
+                cross_recv.at[part, k],
+                other_core,
+            )
+
+    def own(part, after):
+        for number, k in enumerate(blocks):
+            value = product(part, k, core).reshape(2, 8, ROWS, PARTS[part][1])
+            block = piece(from_core.at[k], part)
+            arrive(block, cross_send.at[part, k], cross_recv.at[part, k], other_core)
+            piece(sums.at[k, core], part)[...] = (value + block[...].astype(F32)).astype(BF16)
+            if number in after:
+                after[number]()
+
+    def far_send(part):
+        wide = plus(wide_at[part], 2)
         for side in range(2):
             for k in range(2):
-                wide_send(part, side, 2 * (1 - side) + k)
-    for part in range(2):
-        for side in range(2):
-            near = plus(wide_at[part], 1 if side == 0 else 3)
-            for k in range(2):
+                step = HALVES[side][k]
                 sem = (part, side, k)
-                arrive(
-                    half_one.at[sem],
+                send(
+                    chunk(sums, part, wide, plus(narrow_at[part], step)),
+                    landed(half_one, *sem),
                     half_one_send.at[sem],
                     half_one_recv.at[sem],
                     neighbours[wide_axis[part], side],
                 )
-                add(chunk(sums, part, near, 2 * side + k), half_one.at[sem])
-                wide_send(part, side, 2 * side + k)
+
+    def wide_send(part, side, step):
+        wide = plus(wide_at[part], 1 if side == 0 else 3)
+        sem = (part, side, step)
+        send(
+            chunk(sums, part, wide, plus(narrow_at[part], step)),
+            landed(whole_one, *sem),
+            whole_one_send.at[sem],
+            whole_one_recv.at[sem],
+            neighbours[wide_axis[part], side],
+        )
+
+    def near_send(part):
+        for k in range(2):
+            for side in range(2):
+                wide_send(part, side, HALVES[1 - side][k])
+
+    def near_add(part):
+        for k in range(2):
+            for side in range(2):
+                wide = plus(wide_at[part], 1 if side == 0 else 3)
+                step = HALVES[side][k]
+                sem = (part, side, k)
+                block = landed(half_one, *sem)
+                arrive(
+                    block,
+                    half_one_send.at[sem],
+                    half_one_recv.at[sem],
+                    neighbours[wide_axis[part], side],
+                )
+                add(chunk(sums, part, wide, plus(narrow_at[part], step)), block)
+                wide_send(part, side, step)
+
+    def ahead(side, hop):
+        return lax.rem(z + (hop if side == 0 else 8 - hop), 8)
+
+    def ring_send_sum(hop, side, step):
+        sem = (side, hop - 1, step)
+        send(
+            layer(sums, ahead(side, hop), plus(y, step)),
+            ring_sums.at[sem],
+            ring_sum_send.at[sem],
+            ring_sum_recv.at[sem],
+            along_z[side],
+        )
+
+    def ring_start():
+        for k in range(2):
+            for side in range(2):
+                ring_send_sum(4, side, HALVES[side][k])
+        for k in range(2):
+            for side in range(2):
+                ring_send_sum(3, side, HALVES[1 - side][k])
+
+    def ring_sum(hop):
+        for step in (2, 1, 3, 0):
+            for side in range(2):
+                if hop == 3 and step not in HALVES[side]:
+                    continue
+                sem = (side, hop, step)
+                arrive(
+                    ring_sums.at[sem],
+                    ring_sum_send.at[sem],
+                    ring_sum_recv.at[sem],
+                    along_z[side],
+                )
+                if hop:
+                    add(layer(sums, ahead(side, hop), plus(y, step)), ring_sums.at[sem])
+                    ring_send_sum(hop, side, step)
+            if hop == 0:
+                add(
+                    layer(sums, z, plus(y, step)),
+                    ring_sums.at[0, 0, step],
+                    ring_sums.at[1, 0, step],
+                )
+                if step:
+                    send(
+                        layer(sums, z, plus(y, step)),
+                        y_sums.at[step],
+                        y_sum_send.at[step],
+                        y_sum_recv.at[step],
+                        device(x, plus(y, step), z, core),
+                    )
 
     def narrow_send(part, side):
         near = plus(narrow_at[part], 1 if side == 0 else 3)
         sem = (part, side)
         send(
             chunk(sums, part, wide_at[part], near),
-            whole_two.at[sem],
+            landed(whole_two, *sem),
             whole_two_send.at[sem],
             whole_two_recv.at[sem],
             neighbours[narrow_axis[part], side],
         )
 
-    for step in (2, 1, 3, 0):
-        for part in range(2):
-            narrow = plus(narrow_at[part], step)
+    def wide_add(part, step):
+        narrow = plus(narrow_at[part], step)
+        for side in range(2):
+            sem = (part, side, step)
+            arrive(
+                landed(whole_one, *sem),
+                whole_one_send.at[sem],
+                whole_one_recv.at[sem],
+                neighbours[wide_axis[part], side],
+            )
+        add(
+            chunk(sums, part, wide_at[part], narrow),
+            landed(whole_one, part, 0, step),
+            landed(whole_one, part, 1, step),
+        )
+        if step == 2:
             for side in range(2):
-                sem = (part, side, narrow)
-                arrive(
-                    whole_one.at[sem],
-                    whole_one_send.at[sem],
-                    whole_one_recv.at[sem],
-                    neighbours[wide_axis[part], side],
+                sem = (part, side)
+                send(
+                    chunk(sums, part, wide_at[part], narrow, 4 * side, 4),
+                    landed(half_two, *sem),
+                    half_two_send.at[sem],
+                    half_two_recv.at[sem],
+                    neighbours[narrow_axis[part], side],
                 )
-            add(
-                chunk(sums, part, wide_at[part], narrow),
-                whole_one.at[part, 0, narrow],
-                whole_one.at[part, 1, narrow],
-            )
-            if step == 2:
-                for side in range(2):
-                    sem = (part, side)
-                    send(
-                        chunk(sums, part, wide_at[part], narrow, 2 * side, 2),
-                        half_two.at[sem],
-                        half_two_send.at[sem],
-                        half_two_recv.at[sem],
-                        neighbours[narrow_axis[part], side],
-                    )
-    for part in range(2):
+
+    def narrow_add(part):
         for side in range(2):
             near = plus(narrow_at[part], 1 if side == 0 else 3)
             sem = (part, side)
             arrive(
-                half_two.at[sem],
+                landed(half_two, *sem),
                 half_two_send.at[sem],
                 half_two_recv.at[sem],
                 neighbours[narrow_axis[part], side],
             )
-            add(chunk(sums, part, wide_at[part], near, 2 * side, 2), half_two.at[sem])
+            add(
+                chunk(sums, part, wide_at[part], near, 4 * side, 4), landed(half_two, *sem)
+            )
             narrow_send(part, side)
-    for part in range(2):
+
+    def narrow_end(part):
         for side in range(2):
             sem = (part, side)
             arrive(
-                whole_two.at[sem],
+                landed(whole_two, *sem),
                 whole_two_send.at[sem],
                 whole_two_recv.at[sem],
                 neighbours[narrow_axis[part], side],
             )
         add(
             chunk(sums, part, wide_at[part], narrow_at[part]),
-            whole_two.at[part, 0],
-            whole_two.at[part, 1],
-        )
-    for step in range(1, 8):
-        to = lax.rem(z + step, 8)
+            landed(whole_two, part, 0),
+            landed(whole_two, part, 1),
+        )
+        for step in (4, 3, 5, 2, 6, 1, 7):
+            to = lax.rem(z + step, 8)
+            send(
+                sums.at[c, core, y_hi, to, :, pl.ds(*PARTS[part])],
+                last.at[z, :, pl.ds(*PARTS[part])],
+                last_send.at[part, to],
+                last_recv.at[part, z],
+                device(x, y, to, core),
+            )
+
+    other(0)
+    other(2)
+    own(0, {1: lambda: far_send(0)})
+    near_send(0)
+    own(2, {})
+    ring_start()
+    other(1)
+    near_add(0)
+    own(1, {4: lambda: far_send(1)})
+    near_send(1)
+    ring_sum(3)
+    near_add(1)
+    ring_sum(2)
+    wide_add(0, 2)
+    wide_add(1, 2)
+    ring_sum(1)
+    for step in (1, 3):
+        for part in (1, 0):
+            wide_add(part, step)
+    ring_sum(0)
+    narrow_add(1)
+    narrow_add(0)
+    for part in (1, 0):
+        wide_add(part, 0)
+    for step in (2, 1, 3):
+        arrive(
+            y_sums.at[step],
+            y_sum_send.at[step],
+            y_sum_recv.at[step],
+            device(x, plus(y, 4 - step), z, core),
+        )
+    add(layer(sums, z, y), *(y_sums.at[step] for step in (1, 2, 3)))
+    for step in (2, 1, 3):
         send(
-            sums.at[c, core, y_hi, to],
-            last.at[z],
-            last_send.at[to],
-            last_recv.at[z],
-            device(x, y, to, core),
-        )
-    last[z] = sums[c, core, y_hi, z]
-    for step in range(1, 8):
-        source = lax.rem(z + step, 8)
+            sums.at[y_lo * 4 + plus(x, step), core, y_hi, z, :, pl.ds(*PARTS[2])],
+            x_sums.at[step],
+            x_sum_send.at[step],
+            x_sum_recv.at[step],
+            device(plus(x, step), y, z, core),
+        )
+    narrow_end(1)
+    narrow_end(0)
+    for step in (1, 3, 2):
         arrive(
-            last.at[source],
-            last_send.at[source],
-            last_recv.at[source],
-            device(x, y, source, core),
-        )
-    result = state[...]
-    for k in range(8):
-        result = result + last[k].astype(F32)
-    out_ref[...] = result.astype(BF16)
+            x_sums.at[step],
+            x_sum_send.at[step],
+            x_sum_recv.at[step],
+            device(plus(x, 4 - step), y, z, core),
+        )
+
+    def finish(part, value):
+        lanes = pl.ds(*PARTS[part])
+        value = value + state[:, lanes] + sums[c, core, y_hi, z, :, lanes].astype(F32)
+        out_ref[:, lanes] = value.astype(BF16)
+
+    finish(2, sum(x_sums[step].astype(F32) for step in (1, 2, 3)))
+    for part in (1, 0):
+        value = jnp.zeros((ROWS, PARTS[part][1]), F32)
+        for step in range(1, 8):
+            source = lax.rem(z + step, 8)
+            block = last.at[source, :, pl.ds(*PARTS[part])]
+            arrive(
+                block,
+                last_send.at[part, source],
+                last_recv.at[part, source],
+                device(x, y, source, core),
+            )
+            value = value + block[...].astype(F32)
+        finish(part, value)
 
     for copy in sent:
         copy.wait_send()
-    for part in range(2):
-        for narrow in range(4):
-            block = chunk(rows, part, wide_at[part], narrow)
-            remote(
-                block,
-                block,
-                relay_three_send.at[part, narrow],
-                relay_three_recv.at[part, narrow],
-                neighbours[wide_axis[part], narrow // 2],
-            ).wait_send()
 
     @pl.loop(1, N_EXP)
     def _(step):
@@ -765,8 +1003,9 @@
 ):
     key_width = queries.shape[3]
     pairs = [(N_CTX,), (N_CTX,), (N_EXP,), (N_CTX,), (2,), (8,), (8,), (N_CTX,), (N_EXP,)]
-    pairs += [(8,), (2, 2), (2, 2), (2, 2, 4), (2, 4), (2, 4, 4)]
-    pairs += [(8,), (2, 2, 2), (2, 2, 4), (2, 2), (2, 2), (8,)]
+    pairs += [(8,), (4,), (4,), (2, 2), (2, 2), (2, 2, 4), (2, 4), (2, 4, 4)]
+    pairs += [(2, 4, 4), (8,), (3, 8), (2, 2, 2), (2, 2, 4), (2, 2)]
+    pairs += [(2, 2), (2, 4, 4), (4,), (4,), (2, 8)]
     out = pl.pallas_call(
         layer_kernel,
         out_shape=jax.ShapeDtypeStruct((ROWS, COLS), BF16),
@@ -795,10 +1034,13 @@
             pltpu.VMEM((N_CTX, 2, 2, 8, ROWS, COLS), BF16),
             pltpu.VMEM((N_CTX, 2, 2, 8, ROWS, COLS), BF16),
             pltpu.VMEM((N_CTX, 2, 8, ROWS, COLS), BF16),
-            pltpu.VMEM((2, 2, 2, 4, ROWS, COLS), BF16),
-            pltpu.VMEM((2, 2, 4, 4, ROWS, COLS), BF16),
-            pltpu.VMEM((2, 2, 2, ROWS, COLS), BF16),
-            pltpu.VMEM((2, 2, 4, ROWS, COLS), BF16),
+            pltpu.VMEM((2, 2, 2, 8, ROWS, 384), BF16),
+            pltpu.VMEM((2, 2, 4, 8, ROWS, 384), BF16),
+            pltpu.VMEM((2, 2, 4, ROWS, 384), BF16),
+            pltpu.VMEM((2, 2, 8, ROWS, 384), BF16),
+            pltpu.VMEM((2, 4, 4, 4, ROWS, 256), BF16),
+            pltpu.VMEM((4, 4, ROWS, 256), BF16),
+            pltpu.VMEM((4, ROWS, 256), BF16),
             pltpu.VMEM((8, ROWS, COLS), BF16),
             pltpu.VMEM((2, 256, 128), BF16),
             pltpu.VMEM((N_CTX, COLS, 256), BF16),

time: 140 us -> 137 us (0.979)
  Pallas kernels: 136 us -> 133 us
    pallas_call x1, Pallas kernels: 136 us -> 133 us  [per_device(): pl.pallas_call(layer_kernel, out_shape=jax.ShapeDtypeStruct((ROWS, COLS),...]
where the time goes in v2:
time: 137 us
  Pallas kernels  133 us (97%)
  local copies, waits for them, and re-layouts  2.72 us (2%)
    pallas_call x1, Pallas kernels, per_device(): pl.pallas_call(layer_kernel, out_shape=jax.ShapeDtypeStruct((ROWS, COLS),...  133 us

profile of v2, /device:TPU:1, one launch (start us, length us, event | category | flops | bytes accessed | tf_op | source)
XLA Modules:
  0.0 136.7 jit_solution(9983558213400616941)
XLA Ops:
  0.7 1.4 reshape.36.gain_ref
  2.0 133.3 %layer.1 = bf16[16,896]{1,0:T(8,128)(2,1)} custom-call(s32[1]{0:T(128)S(6)} %copy.22.length_ref, s32[8]{0:T(128)} %bitcast.23, bf16[8,128,576]{2,1,0:T(8,128)(2,1)} %bitcast.16, bf16[576,512]{1,0:T(8,128)(2,1)} %bitcast.17, bf16[16,576]{1,0:T(8,128)(2,1)} %bitcast.20, s32[16,8]{1,0:T(8,128)} %bitcast.21, f32[16,8]{1,0:T(8,128)} %bitcast.22, ...), custom_call_target="tpu_custom_call" | custom-call | tf_op jit(solution)/shard_map/layer/pallas_call | solution.py:1009
  135.3 1.4 copy.23

commit v3 on v2

--- a/solution.py
+++ b/solution.py
@@ -155,8 +155,6 @@
     ring_recv,
     share_send,
     share_recv,
-    share_z_send,
-    share_z_recv,
     cross_send,
     cross_recv,
     half_one_send,
@@ -182,15 +180,20 @@
     def plus(a, k):
         return lax.rem(a + k, 4)
 
+    u, v = x + core * (y - x), y + core * (x - y)
+
+    def at_xy(at_u, at_v):
+        return at_u + core * (at_v - at_u), at_v + core * (at_u - at_v)
+
     neighbours = {
-        ("x", 0): device(plus(x, 1), y, z, core),
-        ("x", 1): device(plus(x, 3), y, z, core),
-        ("y", 0): device(x, plus(y, 1), z, core),
-        ("y", 1): device(x, plus(y, 3), z, core),
+        ("u", 0): device(*at_xy(plus(u, 1), v), z, core),
+        ("u", 1): device(*at_xy(plus(u, 3), v), z, core),
+        ("v", 0): device(*at_xy(u, plus(v, 1)), z, core),
+        ("v", 1): device(*at_xy(u, plus(v, 3)), z, core),
     }
     other_core = device(x, y, z, 1 - core)
-    wide_axis, narrow_axis = ("x", "y"), ("y", "x")
-    wide_at, narrow_at = (x, y), (y, x)
+    wide_axis, narrow_axis = ("u", "v"), ("v", "u")
+    wide_at, narrow_at = (u, v), (v, u)
 
     barrier = pltpu.get_barrier_semaphore()
     for step in range(1, N_CTX):
@@ -213,6 +216,15 @@
         fetch.start()
 
     sent = []
+
+    def taken():
+        copies = list(sent)
+        sent.clear()
+        return copies
+
+    def drain(copies):
+        for copy in copies:
+            copy.wait_send()
 
     def send(source, target_ref, send_sem, recv_sem, target):
         copy = remote(source, target_ref, send_sem, recv_sem, target)
@@ -249,10 +261,13 @@
         send(stat.at[target], got_stat.at[c], stat_send.at[target], stat_recv.at[c], where)
 
     peers = [peer(*k) for k in ((1, 2), (0, 2), (1, 1), (0, 1), (1, 3), (0, 3), (1, 0))]
-    partial(peers[0], part.at[peers[0]], stat.at[peers[0]])
+    early = 4
+    for target in peers[:early]:
+        partial(target, part.at[target], stat.at[target])
     pl.semaphore_wait(barrier, N_CTX - 1 + N_EXP - 1 + 1)
-    send_partial(peers[0])
-    for target in peers[1:]:
+    for target in peers[:early]:
+        send_partial(target)
+    for target in peers[early:]:
         partial(target, part.at[target], stat.at[target])
         send_partial(target)
     partial(c, got.at[c], got_stat.at[c])
@@ -326,9 +341,11 @@
 
     def head_copy(step):
         target = lax.rem(e + step, N_EXP)
-        return remote(
-            heads.at[target], by_head.at[e], head_send.at[target], head_recv.at[e], (c, target)
-        )
+        return remote(heads.at[target], by_head.at[e], head_send, head_recv, (c, target))
+
+    others = pl.ds(0, N_EXP - 1)
+    any_peer = (c, lax.rem(e + 1, N_EXP))
+    all_heads = remote(heads.at[others], by_head.at[others], head_send, head_recv, any_peer)
 
     @pl.loop(1, N_EXP)
     def _(step):
@@ -336,17 +353,7 @@
 
     by_head[e] = heads[e]
 
-    @pl.loop(1, N_EXP)
-    def _(step):
-        source = lax.rem(e + step, N_EXP)
-        remote(
-            heads.at[source],
-            by_head.at[source],
-            head_send.at[source],
-            head_recv.at[source],
-            (c, source),
-        ).wait_recv()
-
+    all_heads.wait_recv()
     latents = dot(orders[1], by_head[...].reshape(512, 128)).astype(BF16)
     halves = []
     for parity in range(2):
@@ -410,7 +417,7 @@
         )
         value = value + from_z[source].astype(F32)
     state[...] = value
-    rows[c, core, y_hi, z] = (value * gain_ref[pl.ds(c, 1), :]).astype(BF16)
+    rows[c, core, y_hi, z] = (value * gain_ref[:, columns]).astype(BF16)
     squares[c] = jnp.broadcast_to(jnp.sum(value * value, axis=-1, keepdims=True), (ROWS, 128))
     for target in peers:
         send(squares.at[c], squares.at[c], square_send.at[target], square_recv.at[c], (target, e))
@@ -418,9 +425,9 @@
     def note_copy(step):
         target = lax.rem(e + step, N_EXP)
         spot = core * 16 + y_hi * 8 + z
-        return remote(
-            notes.at[target], noted.at[spot], note_send.at[target], note_recv.at[spot], (c, target)
-        )
+        return remote(notes.at[target], noted.at[spot], note_send, note_recv, (c, target))
+
+    all_notes = remote(notes.at[others], noted.at[others], note_send, note_recv, any_peer)
 
     def send_notes():
         for source in peers:
@@ -436,7 +443,7 @@
             note_copy(step).start()
 
     def chunk(ref, part, wide, narrow, start=0, count=8):
-        at_x, at_y = (wide, narrow) if part == 0 else (narrow, wide)
+        at_x, at_y = at_xy(wide, narrow) if part == 0 else at_xy(narrow, wide)
         first_lane, lanes = PARTS[part]
         return ref.at[
             lax.rem(at_y, 2) * 4 + at_x,
@@ -469,10 +476,9 @@
             device(plus(x, step), y, z, core),
         )
 
-    def share(part, wide, narrow, step, hop):
+    def share(part, wide, narrow):
         block = chunk(rows, part, wide, narrow)
-        sem = (part, step, hop)
-        send(block, block, share_send.at[sem], share_recv.at[sem], other_core)
+        remote(block, block, share_send.at[part], share_recv.at[part], other_core).start()
 
     def spread(part, step):
         narrow = plus(narrow_at[part], step)
@@ -486,7 +492,7 @@
                 three_recv.at[sem],
                 neighbours[wide_axis[part], side],
             )
-        share(part, wide_at[part], narrow, step, 0)
+        share(part, wide_at[part], narrow)
 
     def spread_z(step):
         block = layer(rows, z, plus(y, step))
@@ -494,9 +500,9 @@
             sem = (side, 0, step)
             send(block, block, ring_send.at[sem], ring_recv.at[sem], along_z[side])
 
-    def share_z(at_z, hop):
+    def share_z(at_z):
         block = rows.at[:, core, :, at_z, :, pl.ds(*PARTS[2])]
-        send(block, block, share_z_send.at[hop], share_z_recv.at[hop], other_core)
+        remote(block, block, share_send.at[2], share_recv.at[2], other_core).start()
 
     for step in (1, 3, 2):
         source = plus(x, 4 - step)
@@ -545,7 +551,7 @@
             device(x, source, z, core),
         )
         spread_z(4 - step)
-    share_z(z, 0)
+    share_z(z)
     for part in range(2):
         for side in range(2):
             step = 3 if side == 0 else 1
@@ -581,9 +587,9 @@
                     send(block, block, ring_send.at[sem], ring_recv.at[sem], along_z[side])
         if hop < 4:
             for side in range(2):
-                share_z(behind(side, hop), 2 * hop - 1 + side)
+                share_z(behind(side, hop))
         else:
-            share_z(behind(0, 4), 7)
+            share_z(behind(0, 4))
 
     def near(step):
         for part in range(2):
@@ -602,7 +608,7 @@
                         relay_three_recv.at[part, step],
                         target,
                     )
-                share(part, wide, narrow, step, 1 + side)
+                share(part, wide, narrow)
 
     near(0)
     ring(1)
@@ -632,44 +638,25 @@
                 relay_three_recv.at[part, step],
                 neighbours[wide_axis[part], side],
             )
-            share(part, wide, narrow, step, 3)
-    for hop in range(8):
-        source = z if hop == 0 else behind(0, 4) if hop == 7 else behind((hop - 1) % 2, (hop + 1) // 2)
-        arrive(
-            rows.at[:, 1 - core, :, source, :, pl.ds(*PARTS[2])],
-            share_z_send.at[hop],
-            share_z_recv.at[hop],
-            other_core,
-        )
-    for part in range(2):
-        first_lane, lanes = PARTS[part]
-        for step in range(4):
-            for hop in range(4):
-                wide = plus(wide_at[part], (0, 3, 1, 2)[hop])
-                narrow = plus(narrow_at[part], step)
-                at_x, at_y = (wide, narrow) if part == 0 else (narrow, wide)
-                block = rows.at[
-                    lax.rem(at_y, 2) * 4 + at_x,
-                    1 - core,
-                    at_y // 2,
-                    :,
-                    :,
-                    pl.ds(first_lane, lanes),
-                ]
-                sem = (part, step, hop)
-                arrive(block, share_send.at[sem], share_recv.at[sem], other_core)
+            share(part, wide, narrow)
+    shared = []
+    for part in range(3):
+        lanes = pl.ds(*PARTS[part])
+        shared.append(
+            remote(
+                rows.at[:, core, :, :, :, lanes],
+                rows.at[:, 1 - core, :, :, :, lanes],
+                share_send.at[part],
+                share_recv.at[part],
+                other_core,
+            )
+        )
+        shared[part].wait_recv()
 
     for fetch in fetches[1:]:
         fetch.wait()
 
-    @pl.loop(1, N_EXP)
-    def _(step):
-        source = lax.rem(e + step, N_EXP)
-        spot = lax.rem(source, 2) * 16 + lax.rem(source // 2, 2) * 8 + source // 4
-        remote(
-            notes.at[source], noted.at[spot], note_send.at[source], note_recv.at[spot], (c, source)
-        ).wait_recv()
-
+    all_notes.wait_recv()
     note = jnp.broadcast_to(noted[...], (N_EXP, ROWS, 128)).reshape(N_EXP * ROWS, 128)
     lane = lax.broadcasted_iota(jnp.int32, (N_EXP * ROWS, 128), 1)
     beam = row_index(N_EXP * ROWS) & 15
@@ -695,9 +682,12 @@
     def piece(ref, part):
         return ref.at[:, :, :, pl.ds(*PARTS[part])]
 
-    blocks = [
-        peer(*k) for k in ((0, 2), (1, 2), (0, 1), (0, 3), (0, 0), (1, 1), (1, 3), (1, 0))
-    ]
+    by_x = [peer(*k) for k in ((0, 2), (1, 2), (0, 1), (0, 3), (0, 0), (1, 1), (1, 3), (1, 0))]
+    by_y = [peer(*k) for k in ((0, 2), (0, 1), (0, 3), (0, 0), (1, 2), (1, 1), (1, 3), (1, 0))]
+
+    def blocks(part, half):
+        by_u, by_v = (by_x, by_y) if part == 0 else (by_y, by_x)
+        return [k + half * (l - k) for k, l in zip(by_u, by_v)]
 
     def product(part, k, half):
         first_lane, lanes = PARTS[part]
@@ -705,7 +695,7 @@
         return dot(hidden[half], down[:, at])
 
     def other(part):
-        for k in blocks:
+        for k in blocks(part, 1 - core):
             block = piece(sums.at[k, 1 - core], part)
             block[...] = (
                 product(part, k, 1 - core).astype(BF16).reshape(2, 8, ROWS, PARTS[part][1])
@@ -719,7 +709,7 @@
             )
 
     def own(part, after):
-        for number, k in enumerate(blocks):
+        for number, k in enumerate(blocks(part, core)):
             value = product(part, k, core).reshape(2, 8, ROWS, PARTS[part][1])
             block = piece(from_core.at[k], part)
             arrive(block, cross_send.at[part, k], cross_recv.at[part, k], other_core)
@@ -900,29 +890,35 @@
                 device(x, y, to, core),
             )
 
+    earlier = taken()
     other(0)
+    own(0, {3: lambda: far_send(0)})
+    near_send(0)
     other(2)
-    own(0, {1: lambda: far_send(0)})
-    near_send(0)
     own(2, {})
     ring_start()
     other(1)
     near_add(0)
-    own(1, {4: lambda: far_send(1)})
+    own(1, {3: lambda: far_send(1)})
     near_send(1)
     ring_sum(3)
     near_add(1)
     ring_sum(2)
+    drain(earlier)
+    all_heads.wait_send()
+    all_notes.wait_send()
+    for copy in shared:
+        copy.wait_send()
     wide_add(0, 2)
+    ring_sum(1)
     wide_add(1, 2)
-    ring_sum(1)
     for step in (1, 3):
-        for part in (1, 0):
+        for part in range(2):
             wide_add(part, step)
     ring_sum(0)
+    narrow_add(0)
     narrow_add(1)
-    narrow_add(0)
-    for part in (1, 0):
+    for part in range(2):
         wide_add(part, 0)
     for step in (2, 1, 3):
         arrive(
@@ -940,8 +936,10 @@
             x_sum_recv.at[step],
             device(plus(x, step), y, z, core),
         )
+    earlier = taken()
+    narrow_end(0)
     narrow_end(1)
-    narrow_end(0)
+    drain(earlier)
     for step in (1, 3, 2):
         arrive(
             x_sums.at[step],
@@ -956,7 +954,7 @@
         out_ref[:, lanes] = value.astype(BF16)
 
     finish(2, sum(x_sums[step].astype(F32) for step in (1, 2, 3)))
-    for part in (1, 0):
+    for part in range(2):
         value = jnp.zeros((ROWS, PARTS[part][1]), F32)
         for step in range(1, 8):
             source = lax.rem(z + step, 8)
@@ -970,13 +968,7 @@
             value = value + block[...].astype(F32)
         finish(part, value)
 
-    for copy in sent:
-        copy.wait_send()
-
-    @pl.loop(1, N_EXP)
-    def _(step):
-        head_copy(step).wait_send()
-        note_copy(step).wait_send()
+    drain(sent)
 
 
 VMEM = pl.BlockSpec(memory_space=pltpu.VMEM)
@@ -1002,10 +994,9 @@
     expert_down,
 ):
     key_width = queries.shape[3]
-    pairs = [(N_CTX,), (N_CTX,), (N_EXP,), (N_CTX,), (2,), (8,), (8,), (N_CTX,), (N_EXP,)]
-    pairs += [(8,), (4,), (4,), (2, 2), (2, 2), (2, 2, 4), (2, 4), (2, 4, 4)]
-    pairs += [(2, 4, 4), (8,), (3, 8), (2, 2, 2), (2, 2, 4), (2, 2)]
-    pairs += [(2, 2), (2, 4, 4), (4,), (4,), (2, 8)]
+    pairs = [(N_CTX,), (N_CTX,), None, (N_CTX,), (2,), (8,), (8,), (N_CTX,), None]
+    pairs += [(8,), (4,), (4,), (2, 2), (2, 2), (2, 2, 4), (2, 4), (2, 4, 4), (3,)]
+    pairs += [(3, 8), (2, 2, 2), (2, 2, 4), (2, 2), (2, 2), (2, 4, 4), (4,), (4,), (2, 8)]
     out = pl.pallas_call(
         layer_kernel,
         out_shape=jax.ShapeDtypeStruct((ROWS, COLS), BF16),
@@ -1047,7 +1038,7 @@
             pltpu.VMEM((128, N_CTX * COLS), BF16),
             DMA((4,)),
         ]
-        + [DMA(shape) for shape in pairs for _ in range(2)],
+        + [DMA(shape) if shape else DMA for shape in pairs for _ in range(2)],
         compiler_params=pltpu.CompilerParams(
             collective_id=0, has_side_effects=True, vmem_limit_bytes=VMEM_LIMIT
         ),
@@ -1063,7 +1054,7 @@
         value_weight,
         output_weight,
         residual.reshape(ROWS, N_CTX * COLS),
-        norm_gain.reshape(N_CTX, COLS),
+        norm_gain.reshape(1, N_CTX * COLS),
         expert_gate.reshape(N_CTX, COLS, 128),
         expert_up.reshape(N_CTX, COLS, 128),
         expert_down[0],

time: 137 us -> 130 us (0.949)
  Pallas kernels: 133 us -> 127 us
    pallas_call x1, Pallas kernels: 133 us -> 127 us  [per_device(): pl.pallas_call(layer_kernel, out_shape=jax.ShapeDtypeStruct((ROWS, COLS),...]
where the time goes in v3:
time: 130 us
  Pallas kernels  127 us (98%)
  local copies, waits for them, and re-layouts  1.36 us (1%)
    pallas_call x1, Pallas kernels, per_device(): pl.pallas_call(layer_kernel, out_shape=jax.ShapeDtypeStruct((ROWS, COLS),...  127 us

profile of v3, /device:TPU:1, one launch (start us, length us, event | category | flops | bytes accessed | tf_op | source)
XLA Modules:
  0.0 129.5 jit_solution(15759684555347940728)
XLA Ops:
  0.7 127.5 %layer.1 = bf16[16,896]{1,0:T(8,128)(2,1)} custom-call(s32[1]{0:T(128)S(6)} %copy.22.length_ref, s32[8]{0:T(128)} %bitcast.25, bf16[8,128,576]{2,1,0:T(8,128)(2,1)} %bitcast.17, bf16[576,512]{1,0:T(8,128)(2,1)} %bitcast.18, bf16[16,576]{1,0:T(8,128)(2,1)} %bitcast.22, s32[16,8]{1,0:T(8,128)} %bitcast.23, f32[16,8]{1,0:T(8,128)} %bitcast.24, ...), custom_call_target="tpu_custom_call" | custom-call | tf_op jit(solution)/shard_map/layer/pallas_call | solution.py:1000
  128.2 1.4 %copy.23 = bf16[2,8,896]{2,1,0:T(8,128)(2,1)} copy(bf16[2,8,896]{2,1,0:T(8,128)(2,1)} %bitcast.20) | data formatting | bytes 57344

commit v4 on v3

--- a/solution.py
+++ b/solution.py
@@ -72,19 +72,24 @@
 def layer_kernel(
     length_ref,
     parents_ref,
-    q_ref,
-    cache_ref,
+    q_hbm,
+    cache_hbm,
     new_ref,
     ids_ref,
     gates_ref,
-    wv_ref,
+    wv_hbm,
     wo_ref,
-    residual_ref,
+    residual_hbm,
     gain_ref,
     gate_ref,
     up_ref,
     down_ref,
     out_ref,
+    q_ref,
+    cache_ref,
+    wv_ref,
+    residual_ref,
+    wo_other,
     part,
     stat,
     got,
@@ -95,8 +100,7 @@
     wo_cols,
     values,
     ordered,
-    crossing,
-    crossed,
+    met,
     shares,
     from_y,
     from_z,
@@ -106,7 +110,6 @@
     noted,
     rows,
     sums,
-    from_core,
     half_one,
     whole_one,
     half_two,
@@ -115,9 +118,12 @@
     y_sums,
     x_sums,
     last,
+    scales,
+    crossing_hidden,
     hidden,
     both,
     down,
+    input_sems,
     weight_sems,
     part_send,
     part_recv,
@@ -155,8 +161,10 @@
     ring_recv,
     share_send,
     share_recv,
-    cross_send,
-    cross_recv,
+    pair_send,
+    pair_recv,
+    hidden_send,
+    hidden_recv,
     half_one_send,
     half_one_recv,
     whole_one_send,
@@ -195,6 +203,12 @@
     wide_axis, narrow_axis = ("u", "v"), ("v", "u")
     wide_at, narrow_at = (u, v), (v, u)
 
+    inputs = [
+        pltpu.make_async_copy(cache_hbm, cache_ref, input_sems.at[0]),
+        pltpu.make_async_copy(q_hbm, q_ref, input_sems.at[1]),
+    ]
+    for fetch in inputs:
+        fetch.start()
     barrier = pltpu.get_barrier_semaphore()
     for step in range(1, N_CTX):
         greet(barrier, (lax.rem(c + step, N_CTX), e))
@@ -210,7 +224,11 @@
         pltpu.make_async_copy(wo_ref.at[:, columns], wo_cols, weight_sems.at[0]),
         pltpu.make_async_copy(gate_ref, both.at[:, :, pl.ds(0, 128)], weight_sems.at[1]),
         pltpu.make_async_copy(up_ref, both.at[:, :, pl.ds(128, 128)], weight_sems.at[2]),
-        pltpu.make_async_copy(down_ref, down, weight_sems.at[3]),
+        pltpu.make_async_copy(
+            down_ref, down.at[pl.ds(pl.multiple_of(core * 128, 128), 128)], weight_sems.at[3]
+        ),
+        pltpu.make_async_copy(wv_hbm, wv_ref, weight_sems.at[4]),
+        pltpu.make_async_copy(residual_hbm.at[:, columns], residual_ref, weight_sems.at[5]),
     ]
     for fetch in fetches:
         fetch.start()
@@ -261,6 +279,8 @@
         send(stat.at[target], got_stat.at[c], stat_send.at[target], stat_recv.at[c], where)
 
     peers = [peer(*k) for k in ((1, 2), (0, 2), (1, 1), (0, 1), (1, 3), (0, 3), (1, 0))]
+    for fetch in inputs:
+        fetch.wait()
     early = 4
     for target in peers[:early]:
         partial(target, part.at[target], stat.at[target])
@@ -270,6 +290,9 @@
     for target in peers[early:]:
         partial(target, part.at[target], stat.at[target])
         send_partial(target)
+    send(wo_ref.at[:, columns], wo_other, pair_send.at[0], pair_recv.at[0], other_core)
+    own_down = down.at[pl.ds(pl.multiple_of(core * 128, 128), 128)]
+    send(down_ref, own_down, pair_send.at[1], pair_recv.at[1], other_core)
     partial(c, got.at[c], got_stat.at[c])
 
     row = row_index(512)
@@ -354,6 +377,7 @@
     by_head[e] = heads[e]
 
     all_heads.wait_recv()
+    fetches[4].wait()
     latents = dot(orders[1], by_head[...].reshape(512, 128)).astype(BF16)
     halves = []
     for parity in range(2):
@@ -371,23 +395,17 @@
     for source in peers:
         arrive(values.at[source], value_send.at[source], value_recv.at[source], (source, e))
     ordered[...] = dot(orders[2], values[...].reshape(512, 256)).astype(BF16).reshape(2, 256, 256)
+    send(ordered.at[1 - core], met, crossing_send, crossing_recv, other_core)
     fetches[0].wait()
-    crossing[...] = dot(ordered[1 - core], wo_cols[...]).astype(BF16).reshape(2, 8, ROWS, COLS)
-    for half in (1, 0):
-        at = lax.rem(y_hi + half, 2)
-        send(
-            crossing.at[at],
-            crossed.at[at],
-            crossing_send.at[at],
-            crossing_recv.at[at],
-            other_core,
-        )
+    arrive(wo_other, pair_send.at[0], pair_recv.at[0], other_core)
     other_y = device(x, plus(y, 2), z, core)
     for half in (1, 0):
         at = lax.rem(y_hi + half, 2)
-        own = dot(ordered[core, pl.ds(pl.multiple_of(at * 128, 128), 128)], wo_cols[...])
-        arrive(crossed.at[at], crossing_send.at[at], crossing_recv.at[at], other_core)
-        own = own + crossed[at].reshape(128, COLS).astype(F32)
+        near_rows = pl.ds(pl.multiple_of(at * 128, 128), 128)
+        own = dot(ordered[core, near_rows], wo_cols[...])
+        if half:
+            arrive(met, crossing_send, crossing_recv, other_core)
+        own = own + dot(met[near_rows], wo_other[...])
         shares[at] = own.astype(BF16).reshape(8, ROWS, COLS)
         if half:
             for step in (4, 3, 5, 2, 6, 1, 7, 0):
@@ -406,7 +424,8 @@
                 zsum_recv.at[z],
                 device(x, y, to, core),
             )
-    value = residual_ref[:, columns].astype(F32) + both_y
+    fetches[5].wait()
+    value = residual_ref[...].astype(F32) + both_y
     for step in range(1, 8):
         source = lax.rem(z + step, 8)
         arrive(
@@ -445,17 +464,12 @@
     def chunk(ref, part, wide, narrow, start=0, count=8):
         at_x, at_y = at_xy(wide, narrow) if part == 0 else at_xy(narrow, wide)
         first_lane, lanes = PARTS[part]
-        return ref.at[
-            lax.rem(at_y, 2) * 4 + at_x,
-            core,
-            at_y // 2,
-            pl.ds(start, count),
-            :,
-            pl.ds(first_lane, lanes),
-        ]
+        at = (lax.rem(at_y, 2) * 4 + at_x,) + ((core,) if ref is rows else ())
+        return ref.at[at + (at_y // 2, pl.ds(start, count), slice(None), pl.ds(first_lane, lanes))]
 
     def layer(ref, at_z, at_y):
-        return ref.at[pl.ds(lax.rem(at_y, 2) * 4, 4), core, at_y // 2, at_z, :, pl.ds(*PARTS[2])]
+        at = (pl.ds(lax.rem(at_y, 2) * 4, 4),) + ((core,) if ref is rows else ())
+        return ref.at[at + (at_y // 2, at_z, slice(None), pl.ds(*PARTS[2]))]
 
     along_z = (device(x, y, lax.rem(z + 1, 8), core), device(x, y, lax.rem(z + 7, 8), core))
 
@@ -653,7 +667,7 @@
         )
         shared[part].wait_recv()
 
-    for fetch in fetches[1:]:
+    for fetch in fetches[1:4]:
         fetch.wait()
 
     all_notes.wait_recv()
@@ -662,13 +676,33 @@
     beam = row_index(N_EXP * ROWS) & 15
     routed = jnp.sum(jnp.where(lane == beam, note, 0.0), axis=-1, keepdims=True)
     scale = jnp.sum(jnp.where(lane == beam + 16, note, 0.0), axis=-1, keepdims=True)
-    total = jnp.zeros((512, 256), F32)
-    for k in range(N_CTX):
-        total = total + dot(rows[k].reshape(512, COLS), both[k])
-    total = total * scale
-    gate, up = total[:, :128], total[:, 128:]
-    silu = gate / (1.0 + jnp.exp(-gate))
-    hidden[...] = (silu * up * routed).astype(BF16).reshape(2, 256, 128)
+    def hide(half):
+        total = jnp.zeros((256, 256), F32)
+        for k in range(N_CTX):
+            total = total + dot(rows[k, half].reshape(256, COLS), both[k])
+        rows_at = pl.ds(pl.multiple_of(half * 256, 256), 256)
+        total = total * scales[rows_at, :1]
+        gate, up = total[:, :128], total[:, 128:]
+        silu = gate / (1.0 + jnp.exp(-gate))
+        return (silu * up * scales[rows_at, 1:2]).astype(BF16)
+
+    def lanes_of(half):
+        return pl.ds(pl.multiple_of(half * 128, 128), 128)
+
+    scales[...] = jnp.where(lane == 0, scale, routed)
+    crossing_hidden[...] = hide(1 - core)
+    send(
+        crossing_hidden,
+        hidden.at[:, lanes_of(core)],
+        hidden_send,
+        hidden_recv,
+        other_core,
+    )
+    hidden[:, lanes_of(core)] = hide(core)
+    other_lanes = hidden.at[:, lanes_of(1 - core)]
+    arrive(other_lanes, hidden_send, hidden_recv, other_core)
+    other_down = down.at[pl.ds(pl.multiple_of((1 - core) * 128, 128), 128)]
+    arrive(other_down, pair_send.at[1], pair_recv.at[1], other_core)
 
     def add(ref, *others):
         value = ref[...].astype(F32)
@@ -685,35 +719,18 @@
     by_x = [peer(*k) for k in ((0, 2), (1, 2), (0, 1), (0, 3), (0, 0), (1, 1), (1, 3), (1, 0))]
     by_y = [peer(*k) for k in ((0, 2), (0, 1), (0, 3), (0, 0), (1, 2), (1, 1), (1, 3), (1, 0))]
 
-    def blocks(part, half):
+    def blocks(part):
         by_u, by_v = (by_x, by_y) if part == 0 else (by_y, by_x)
-        return [k + half * (l - k) for k, l in zip(by_u, by_v)]
-
-    def product(part, k, half):
+        return [k + core * (l - k) for k, l in zip(by_u, by_v)]
+
+    def product(part, k):
         first_lane, lanes = PARTS[part]
         at = pl.ds(pl.multiple_of(k * COLS + first_lane, 128), lanes)
-        return dot(hidden[half], down[:, at])
-
-    def other(part):
-        for k in blocks(part, 1 - core):
-            block = piece(sums.at[k, 1 - core], part)
-            block[...] = (
-                product(part, k, 1 - core).astype(BF16).reshape(2, 8, ROWS, PARTS[part][1])
-            )
-            send(
-                block,
-                piece(from_core.at[k], part),
-                cross_send.at[part, k],
-                cross_recv.at[part, k],
-                other_core,
-            )
+        return dot(hidden[...], down[:, at]).astype(BF16).reshape(2, 8, ROWS, lanes)
 
     def own(part, after):
-        for number, k in enumerate(blocks(part, core)):
-            value = product(part, k, core).reshape(2, 8, ROWS, PARTS[part][1])
-            block = piece(from_core.at[k], part)
-            arrive(block, cross_send.at[part, k], cross_recv.at[part, k], other_core)
-            piece(sums.at[k, core], part)[...] = (value + block[...].astype(F32)).astype(BF16)
+        for number, k in enumerate(blocks(part)):
+            piece(sums.at[k], part)[...] = product(part, k)
             if number in after:
                 after[number]()
 
@@ -883,7 +900,7 @@
         for step in (4, 3, 5, 2, 6, 1, 7):
             to = lax.rem(z + step, 8)
             send(
-                sums.at[c, core, y_hi, to, :, pl.ds(*PARTS[part])],
+                sums.at[c, y_hi, to, :, pl.ds(*PARTS[part])],
                 last.at[z, :, pl.ds(*PARTS[part])],
                 last_send.at[part, to],
                 last_recv.at[part, z],
@@ -891,16 +908,13 @@
             )
 
     earlier = taken()
-    other(0)
     own(0, {3: lambda: far_send(0)})
     near_send(0)
-    other(2)
     own(2, {})
     ring_start()
-    other(1)
-    near_add(0)
     own(1, {3: lambda: far_send(1)})
     near_send(1)
+    near_add(0)
     ring_sum(3)
     near_add(1)
     ring_sum(2)
@@ -915,9 +929,9 @@
     for step in (1, 3):
         for part in range(2):
             wide_add(part, step)
-    ring_sum(0)
     narrow_add(0)
     narrow_add(1)
+    ring_sum(0)
     for part in range(2):
         wide_add(part, 0)
     for step in (2, 1, 3):
@@ -930,7 +944,7 @@
     add(layer(sums, z, y), *(y_sums.at[step] for step in (1, 2, 3)))
     for step in (2, 1, 3):
         send(
-            sums.at[y_lo * 4 + plus(x, step), core, y_hi, z, :, pl.ds(*PARTS[2])],
+            sums.at[y_lo * 4 + plus(x, step), y_hi, z, :, pl.ds(*PARTS[2])],
             x_sums.at[step],
             x_sum_send.at[step],
             x_sum_recv.at[step],
@@ -950,7 +964,7 @@
 
     def finish(part, value):
         lanes = pl.ds(*PARTS[part])
-        value = value + state[:, lanes] + sums[c, core, y_hi, z, :, lanes].astype(F32)
+        value = value + state[:, lanes] + sums[c, y_hi, z, :, lanes].astype(F32)
         out_ref[:, lanes] = value.astype(BF16)
 
     finish(2, sum(x_sums[step].astype(F32) for step in (1, 2, 3)))
@@ -994,15 +1008,20 @@
     expert_down,
 ):
     key_width = queries.shape[3]
-    pairs = [(N_CTX,), (N_CTX,), None, (N_CTX,), (2,), (8,), (8,), (N_CTX,), None]
+    pairs = [(N_CTX,), (N_CTX,), None, (N_CTX,), None, (8,), (8,), (N_CTX,), None]
     pairs += [(8,), (4,), (4,), (2, 2), (2, 2), (2, 2, 4), (2, 4), (2, 4, 4), (3,)]
-    pairs += [(3, 8), (2, 2, 2), (2, 2, 4), (2, 2), (2, 2), (2, 4, 4), (4,), (4,), (2, 8)]
+    pairs += [(2,), None, (2, 2, 2), (2, 2, 4), (2, 2), (2, 2), (2, 4, 4), (4,), (4,), (2, 8)]
     out = pl.pallas_call(
         layer_kernel,
         out_shape=jax.ShapeDtypeStruct((ROWS, COLS), BF16),
-        in_specs=[SMEM, SMEM] + [VMEM] * 6 + [ANY, VMEM, VMEM, ANY, ANY, ANY],
+        in_specs=[SMEM, SMEM, ANY, ANY, VMEM, VMEM, VMEM, ANY, ANY, ANY, VMEM, ANY, ANY, ANY],
         out_specs=VMEM,
         scratch_shapes=[
+            pltpu.VMEM((N_CTX, 128, key_width), BF16),
+            pltpu.VMEM((key_width, prompt_cache.shape[1]), BF16),
+            pltpu.VMEM(value_weight.shape, BF16),
+            pltpu.VMEM((ROWS, COLS), BF16),
+            pltpu.VMEM((256, COLS), BF16),
             pltpu.VMEM((N_CTX, 128, LAT), BF16),
             pltpu.VMEM((N_CTX, 8, 128), F32),
             pltpu.VMEM((N_CTX, 128, LAT), BF16),
@@ -1013,8 +1032,7 @@
             pltpu.VMEM((256, COLS), BF16),
             pltpu.VMEM((N_CTX, 64, 256), BF16),
             pltpu.VMEM((2, 256, 256), BF16),
-            pltpu.VMEM((2, 8, ROWS, COLS), BF16),
-            pltpu.VMEM((2, 8, ROWS, COLS), BF16),
+            pltpu.VMEM((256, 256), BF16),
             pltpu.VMEM((2, 8, ROWS, COLS), BF16),
             pltpu.VMEM((8, ROWS, COLS), BF16),
             pltpu.VMEM((8, ROWS, COLS), BF16),
@@ -1022,7 +1040,6 @@
             pltpu.VMEM((ROWS, COLS), F32),
             pltpu.VMEM((N_EXP, 1, 128), F32),
             pltpu.VMEM((N_EXP, 1, 128), F32),
-            pltpu.VMEM((N_CTX, 2, 2, 8, ROWS, COLS), BF16),
             pltpu.VMEM((N_CTX, 2, 2, 8, ROWS, COLS), BF16),
             pltpu.VMEM((N_CTX, 2, 8, ROWS, COLS), BF16),
             pltpu.VMEM((2, 2, 2, 8, ROWS, 384), BF16),
@@ -1033,10 +1050,13 @@
             pltpu.VMEM((4, 4, ROWS, 256), BF16),
             pltpu.VMEM((4, ROWS, 256), BF16),
             pltpu.VMEM((8, ROWS, COLS), BF16),
-            pltpu.VMEM((2, 256, 128), BF16),
+            pltpu.VMEM((512, 128), F32),
+            pltpu.VMEM((256, 128), BF16),
+            pltpu.VMEM((256, 256), BF16),
             pltpu.VMEM((N_CTX, COLS, 256), BF16),
-            pltpu.VMEM((128, N_CTX * COLS), BF16),
-            DMA((4,)),
+            pltpu.VMEM((256, N_CTX * COLS), BF16),
+            DMA((2,)),
+            DMA((6,)),
         ]
         + [DMA(shape) if shape else DMA for shape in pairs for _ in range(2)],
         compiler_params=pltpu.CompilerParams(

time: 130 us -> 123 us (0.946)
  Pallas kernels: 127 us -> 120 us
    pallas_call x1, Pallas kernels: 127 us -> 120 us  [per_device(): pl.pallas_call(layer_kernel, out_shape=jax.ShapeDtypeStruct((ROWS, COLS),...]
where the time goes in v4:
time: 123 us; the launch traced here: 122 us
  Pallas kernels  120 us (98%)
  local copies, waits for them, and re-layouts  1.36 us (1%)
    pallas_call x1, Pallas kernels, per_device(): pl.pallas_call(layer_kernel, out_shape=jax.ShapeDtypeStruct((ROWS, COLS),...  120 us

profile of v4, /device:TPU:1, one launch (start us, length us, event | category | flops | bytes accessed | tf_op | source)
XLA Modules:
  0.0 122.3 jit_solution(12964046261122694075)
XLA Ops:
  0.7 120.3 %layer.1 = bf16[16,896]{1,0:T(8,128)(2,1)} custom-call(s32[1]{0:T(128)S(6)} %copy.22.length_ref, s32[8]{0:T(128)} %bitcast.25, bf16[8,128,576]{2,1,0:T(8,128)(2,1)} %bitcast.17, bf16[576,512]{1,0:T(8,128)(2,1)} %bitcast.18, bf16[16,576]{1,0:T(8,128)(2,1)} %bitcast.22, s32[16,8]{1,0:T(8,128)} %bitcast.23, f32[16,8]{1,0:T(8,128)} %bitcast.24, ...), custom_call_target="tpu_custom_call" | custom-call | tf_op jit(solution)/shard_map/layer/pallas_call | solution.py:1014
  121.0 1.4 %copy.23 = bf16[2,8,896]{2,1,0:T(8,128)(2,1)} copy(bf16[2,8,896]{2,1,0:T(8,128)(2,1)} %bitcast.20) | data formatting | bytes 57344

commit v5 on v4

--- a/solution.py
+++ b/solution.py
@@ -112,11 +112,9 @@
     sums,
     half_one,
     whole_one,
-    half_two,
     whole_two,
     ring_sums,
-    y_sums,
-    x_sums,
+    xy_sums,
     last,
     scales,
     crossing_hidden,
@@ -145,14 +143,10 @@
     note_recv,
     z_send,
     z_recv,
-    x_send,
-    x_recv,
-    y_row_send,
-    y_row_recv,
+    xy_send,
+    xy_recv,
     two_send,
     two_recv,
-    relay_two_send,
-    relay_two_recv,
     three_send,
     three_recv,
     relay_three_send,
@@ -169,16 +163,12 @@
     half_one_recv,
     whole_one_send,
     whole_one_recv,
-    half_two_send,
-    half_two_recv,
     whole_two_send,
     whole_two_recv,
     ring_sum_send,
     ring_sum_recv,
-    y_sum_send,
-    y_sum_recv,
-    x_sum_send,
-    x_sum_recv,
+    xy_sum_send,
+    xy_sum_recv,
     last_send,
     last_recv,
 ):
@@ -198,6 +188,8 @@
         ("u", 1): device(*at_xy(plus(u, 3), v), z, core),
         ("v", 0): device(*at_xy(u, plus(v, 1)), z, core),
         ("v", 1): device(*at_xy(u, plus(v, 3)), z, core),
+        ("u", 2): device(*at_xy(plus(u, 2), v), z, core),
+        ("v", 2): device(*at_xy(u, plus(v, 2)), z, core),
     }
     other_core = device(x, y, z, 1 - core)
     wide_axis, narrow_axis = ("u", "v"), ("v", "u")
@@ -217,7 +209,8 @@
     def _(step):
         greet(barrier, (c, lax.rem(e + step, N_EXP)))
 
-    greet(barrier, device(x, 3 - y, z, core))
+    for step in range(1, N_CTX):
+        greet(barrier, (lax.rem(c + step, N_CTX), e + 2 - 4 * y_hi))
 
     columns = pl.ds(pl.multiple_of(c * COLS, 128), COLS)
     fetches = [
@@ -284,7 +277,7 @@
     early = 4
     for target in peers[:early]:
         partial(target, part.at[target], stat.at[target])
-    pl.semaphore_wait(barrier, N_CTX - 1 + N_EXP - 1 + 1)
+    pl.semaphore_wait(barrier, 2 * (N_CTX - 1) + N_EXP - 1)
     for target in peers[:early]:
         send_partial(target)
     for target in peers[early:]:
@@ -481,14 +474,16 @@
         block = rows.at[c, core, y_hi, z, :, pl.ds(0, PARTS[2][0])]
         send(block, block, z_send.at[to], z_recv.at[z], device(x, y, to, core))
     block = rows.at[c, core, y_hi, z, :, pl.ds(*PARTS[2])]
-    for step in (2, 1, 3):
-        send(
-            block,
-            block,
-            x_send.at[step],
-            x_recv.at[step],
-            device(plus(x, step), y, z, core),
-        )
+    for dy in range(4):
+        for dx in range(4):
+            if dx or dy:
+                send(
+                    block,
+                    block,
+                    xy_send.at[4 * dy + dx],
+                    xy_recv.at[4 * dy + dx],
+                    device(plus(x, dx), plus(y, dy), z, core),
+                )
 
     def share(part, wide, narrow):
         block = chunk(rows, part, wide, narrow)
@@ -518,23 +513,20 @@
         block = rows.at[:, core, :, at_z, :, pl.ds(*PARTS[2])]
         remote(block, block, share_send.at[2], share_recv.at[2], other_core).start()
 
-    for step in (1, 3, 2):
-        source = plus(x, 4 - step)
-        arrive(
-            rows.at[y_lo * 4 + source, core, y_hi, z, :, pl.ds(*PARTS[2])],
-            x_send.at[step],
-            x_recv.at[step],
-            device(source, y, z, core),
-        )
-    block = layer(rows, z, y)
-    for step in (2, 1, 3):
-        send(
-            block,
-            block,
-            y_row_send.at[step],
-            y_row_recv.at[step],
-            device(x, plus(y, step), z, core),
-        )
+    def arrive_plane(dy):
+        for dx in range(4):
+            if dx or dy:
+                at_x, at_y = plus(x, 4 - dx), plus(y, 4 - dy)
+                arrive(
+                    rows.at[
+                        lax.rem(at_y, 2) * 4 + at_x, core, at_y // 2, z, :, pl.ds(*PARTS[2])
+                    ],
+                    xy_send.at[4 * dy + dx],
+                    xy_recv.at[4 * dy + dx],
+                    device(at_x, at_y, z, core),
+                )
+
+    arrive_plane(0)
     spread_z(0)
     for step in range(1, 8):
         source = lax.rem(z + step, 8)
@@ -546,7 +538,7 @@
         )
     for part in range(2):
         block = chunk(rows, part, wide_at[part], narrow_at[part])
-        for side in range(2):
+        for side in range(3):
             send(
                 block,
                 block,
@@ -556,36 +548,24 @@
             )
     for part in range(2):
         spread(part, 0)
-    for step in (1, 3, 2):
-        source = plus(y, 4 - step)
-        arrive(
-            layer(rows, z, source),
-            y_row_send.at[step],
-            y_row_recv.at[step],
-            device(x, source, z, core),
-        )
-        spread_z(4 - step)
+    for dy in (1, 3, 2):
+        arrive_plane(dy)
+        spread_z(4 - dy)
     share_z(z)
-    for part in range(2):
-        for side in range(2):
-            step = 3 if side == 0 else 1
-            near = plus(narrow_at[part], step)
-            target = neighbours[narrow_axis[part], side]
+
+    def arrive_narrow(side):
+        step = (3, 1, 2)[side]
+        for part in range(2):
             arrive(
-                chunk(rows, part, wide_at[part], near),
+                chunk(rows, part, wide_at[part], plus(narrow_at[part], step)),
                 two_send.at[part, side],
                 two_recv.at[part, side],
-                target,
-            )
-            block = chunk(rows, part, wide_at[part], near, 4 * side, 4)
-            send(
-                block,
-                block,
-                relay_two_send.at[part, side],
-                relay_two_recv.at[part, side],
-                target,
+                neighbours[narrow_axis[part], side],
             )
             spread(part, step)
+
+    arrive_narrow(0)
+    arrive_narrow(1)
     send_notes()
 
     def ring(hop):
@@ -626,16 +606,7 @@
 
     near(0)
     ring(1)
-    for part in range(2):
-        far = plus(narrow_at[part], 2)
-        for side in range(2):
-            arrive(
-                chunk(rows, part, wide_at[part], far, 4 * side, 4),
-                relay_two_send.at[part, side],
-                relay_two_recv.at[part, side],
-                neighbours[narrow_axis[part], side],
-            )
-        spread(part, 2)
+    arrive_narrow(2)
     near(3)
     near(1)
     ring(2)
@@ -822,25 +793,22 @@
                     ring_sums.at[0, 0, step],
                     ring_sums.at[1, 0, step],
                 )
-                if step:
-                    send(
-                        layer(sums, z, plus(y, step)),
-                        y_sums.at[step],
-                        y_sum_send.at[step],
-                        y_sum_recv.at[step],
-                        device(x, plus(y, step), z, core),
-                    )
-
-    def narrow_send(part, side):
-        near = plus(narrow_at[part], 1 if side == 0 else 3)
-        sem = (part, side)
-        send(
-            chunk(sums, part, wide_at[part], near),
-            landed(whole_two, *sem),
-            whole_two_send.at[sem],
-            whole_two_recv.at[sem],
-            neighbours[narrow_axis[part], side],
-        )
+                at_y = plus(y, step)
+                for dx in range(4):
+                    if dx or step:
+                        send(
+                            sums.at[
+                                lax.rem(at_y, 2) * 4 + plus(x, dx),
+                                at_y // 2,
+                                z,
+                                :,
+                                pl.ds(*PARTS[2]),
+                            ],
+                            xy_sums.at[4 * step + dx],
+                            xy_sum_send.at[4 * step + dx],
+                            xy_sum_recv.at[4 * step + dx],
+                            device(plus(x, dx), at_y, z, core),
+                        )
 
     def wide_add(part, step):
         narrow = plus(narrow_at[part], step)
@@ -857,46 +825,25 @@
             landed(whole_one, part, 0, step),
             landed(whole_one, part, 1, step),
         )
-        if step == 2:
-            for side in range(2):
-                sem = (part, side)
-                send(
-                    chunk(sums, part, wide_at[part], narrow, 4 * side, 4),
-                    landed(half_two, *sem),
-                    half_two_send.at[sem],
-                    half_two_recv.at[sem],
-                    neighbours[narrow_axis[part], side],
-                )
-
-    def narrow_add(part):
-        for side in range(2):
-            near = plus(narrow_at[part], 1 if side == 0 else 3)
-            sem = (part, side)
+        if step:
+            send(
+                chunk(sums, part, wide_at[part], narrow),
+                landed(whole_two, part, step - 1),
+                whole_two_send.at[part, step - 1],
+                whole_two_recv.at[part, step - 1],
+                neighbours[narrow_axis[part], (0, 2, 1)[step - 1]],
+            )
+
+    def narrow_end(part):
+        blocks_here = [landed(whole_two, part, k) for k in range(3)]
+        for k in range(3):
             arrive(
-                landed(half_two, *sem),
-                half_two_send.at[sem],
-                half_two_recv.at[sem],
-                neighbours[narrow_axis[part], side],
-            )
-            add(
-                chunk(sums, part, wide_at[part], near, 4 * side, 4), landed(half_two, *sem)
-            )
-            narrow_send(part, side)
-
-    def narrow_end(part):
-        for side in range(2):
-            sem = (part, side)
-            arrive(
-                landed(whole_two, *sem),
-                whole_two_send.at[sem],
-                whole_two_recv.at[sem],
-                neighbours[narrow_axis[part], side],
-            )
-        add(
-            chunk(sums, part, wide_at[part], narrow_at[part]),
-            landed(whole_two, part, 0),
-            landed(whole_two, part, 1),
-        )
+                blocks_here[k],
+                whole_two_send.at[part, k],
+                whole_two_recv.at[part, k],
+                neighbours[narrow_axis[part], k],
+            )
+        add(chunk(sums, part, wide_at[part], narrow_at[part]), *blocks_here)
         for step in (4, 3, 5, 2, 6, 1, 7):
             to = lax.rem(z + step, 8)
             send(
@@ -926,40 +873,21 @@
     wide_add(0, 2)
     ring_sum(1)
     wide_add(1, 2)
-    for step in (1, 3):
+    for step in (1, 3, 0):
         for part in range(2):
             wide_add(part, step)
-    narrow_add(0)
-    narrow_add(1)
     ring_sum(0)
-    for part in range(2):
-        wide_add(part, 0)
-    for step in (2, 1, 3):
-        arrive(
-            y_sums.at[step],
-            y_sum_send.at[step],
-            y_sum_recv.at[step],
-            device(x, plus(y, 4 - step), z, core),
-        )
-    add(layer(sums, z, y), *(y_sums.at[step] for step in (1, 2, 3)))
-    for step in (2, 1, 3):
-        send(
-            sums.at[y_lo * 4 + plus(x, step), y_hi, z, :, pl.ds(*PARTS[2])],
-            x_sums.at[step],
-            x_sum_send.at[step],
-            x_sum_recv.at[step],
-            device(plus(x, step), y, z, core),
-        )
     earlier = taken()
     narrow_end(0)
     narrow_end(1)
     drain(earlier)
-    for step in (1, 3, 2):
+    for k in range(1, 16):
+        dy, dx = k // 4, k % 4
         arrive(
-            x_sums.at[step],
-            x_sum_send.at[step],
-            x_sum_recv.at[step],
-            device(plus(x, 4 - step), y, z, core),
+            xy_sums.at[k],
+            xy_sum_send.at[k],
+            xy_sum_recv.at[k],
+            device(plus(x, 4 - dx), plus(y, 4 - dy), z, core),
         )
 
     def finish(part, value):
@@ -967,7 +895,7 @@
         value = value + state[:, lanes] + sums[c, y_hi, z, :, lanes].astype(F32)
         out_ref[:, lanes] = value.astype(BF16)
 
-    finish(2, sum(x_sums[step].astype(F32) for step in (1, 2, 3)))
+    finish(2, sum(xy_sums[k].astype(F32) for k in range(1, 16)))
     for part in range(2):
         value = jnp.zeros((ROWS, PARTS[part][1]), F32)
         for step in range(1, 8):
@@ -1009,8 +937,8 @@
 ):
     key_width = queries.shape[3]
     pairs = [(N_CTX,), (N_CTX,), None, (N_CTX,), None, (8,), (8,), (N_CTX,), None]
-    pairs += [(8,), (4,), (4,), (2, 2), (2, 2), (2, 2, 4), (2, 4), (2, 4, 4), (3,)]
-    pairs += [(2,), None, (2, 2, 2), (2, 2, 4), (2, 2), (2, 2), (2, 4, 4), (4,), (4,), (2, 8)]
+    pairs += [(8,), (16,), (2, 3), (2, 2, 4), (2, 4), (2, 4, 4), (3,)]
+    pairs += [(2,), None, (2, 2, 2), (2, 2, 4), (2, 3), (2, 4, 4), (16,), (2, 8)]
     out = pl.pallas_call(
         layer_kernel,
         out_shape=jax.ShapeDtypeStruct((ROWS, COLS), BF16),
@@ -1044,11 +972,9 @@
             pltpu.VMEM((N_CTX, 2, 8, ROWS, COLS), BF16),
             pltpu.VMEM((2, 2, 2, 8, ROWS, 384), BF16),
             pltpu.VMEM((2, 2, 4, 8, ROWS, 384), BF16),
-            pltpu.VMEM((2, 2, 4, ROWS, 384), BF16),
-            pltpu.VMEM((2, 2, 8, ROWS, 384), BF16),
+            pltpu.VMEM((2, 3, 8, ROWS, 384), BF16),
             pltpu.VMEM((2, 4, 4, 4, ROWS, 256), BF16),
-            pltpu.VMEM((4, 4, ROWS, 256), BF16),
-            pltpu.VMEM((4, ROWS, 256), BF16),
+            pltpu.VMEM((16, ROWS, 256), BF16),
             pltpu.VMEM((8, ROWS, COLS), BF16),
             pltpu.VMEM((512, 128), F32),
             pltpu.VMEM((256, 128), BF16),

time: 123 us -> 121 us (0.984)
    pallas_call x1, Pallas kernels: 120 us -> 119 us  [per_device(): pl.pallas_call(layer_kernel, out_shape=jax.ShapeDtypeStruct((ROWS, COLS),...]
where the time goes in v5:
time: 121 us
  Pallas kernels  119 us (98%)
  local copies, waits for them, and re-layouts  1.36 us (1%)
    pallas_call x1, Pallas kernels, per_device(): pl.pallas_call(layer_kernel, out_shape=jax.ShapeDtypeStruct((ROWS, COLS),...  119 us

profile of v5, /device:TPU:1, one launch (start us, length us, event | category | flops | bytes accessed | tf_op | source)
XLA Modules:
  0.0 120.6 jit_solution(8430593085196913972)
XLA Ops:
  0.7 118.6 %layer.1 = bf16[16,896]{1,0:T(8,128)(2,1)} custom-call(s32[1]{0:T(128)S(6)} %copy.22.length_ref, s32[8]{0:T(128)} %bitcast.25, bf16[8,128,576]{2,1,0:T(8,128)(2,1)} %bitcast.17, bf16[576,512]{1,0:T(8,128)(2,1)} %bitcast.18, bf16[16,576]{1,0:T(8,128)(2,1)} %bitcast.22, s32[16,8]{1,0:T(8,128)} %bitcast.23, f32[16,8]{1,0:T(8,128)} %bitcast.24, ...), custom_call_target="tpu_custom_call" | custom-call | tf_op jit(solution)/shard_map/layer/pallas_call | solution.py:942
  119.3 1.4 %copy.23 = bf16[2,8,896]{2,1,0:T(8,128)(2,1)} copy(bf16[2,8,896]{2,1,0:T(8,128)(2,1)} %bitcast.20) | data formatting | bytes 57344

commit v6 on v5

--- a/solution.py
+++ b/solution.py
@@ -266,10 +266,11 @@
     def peer(flip, step):
         return lax.rem(y_lo + flip, 2) * 4 + plus(x, step)
 
-    def send_partial(target):
+    def send_partial(k):
+        target = peers[k]
         where = (target, e)
-        send(part.at[target], got.at[c], part_send.at[target], part_recv.at[c], where)
-        send(stat.at[target], got_stat.at[c], stat_send.at[target], stat_recv.at[c], where)
+        send(stat.at[target], got_stat.at[k], stat_send.at[k], stat_recv.at[k], where)
+        send(part.at[target], got.at[k], part_send.at[k], part_recv.at[k], where)
 
     peers = [peer(*k) for k in ((1, 2), (0, 2), (1, 1), (0, 1), (1, 3), (0, 3), (1, 0))]
     for fetch in inputs:
@@ -278,15 +279,15 @@
     for target in peers[:early]:
         partial(target, part.at[target], stat.at[target])
     pl.semaphore_wait(barrier, 2 * (N_CTX - 1) + N_EXP - 1)
-    for target in peers[:early]:
-        send_partial(target)
-    for target in peers[early:]:
-        partial(target, part.at[target], stat.at[target])
-        send_partial(target)
+    for k in range(early):
+        send_partial(k)
+    for k in range(early, N_CTX - 1):
+        partial(peers[k], part.at[peers[k]], stat.at[peers[k]])
+        send_partial(k)
     send(wo_ref.at[:, columns], wo_other, pair_send.at[0], pair_recv.at[0], other_core)
     own_down = down.at[pl.ds(pl.multiple_of(core * 128, 128), 128)]
     send(down_ref, own_down, pair_send.at[1], pair_recv.at[1], other_core)
-    partial(c, got.at[c], got_stat.at[c])
+    partial(c, got.at[N_CTX - 1], got_stat.at[N_CTX - 1])
 
     row = row_index(512)
     orders[0] = one_hot(
@@ -333,9 +334,8 @@
     for k in range(8):
         dense = jnp.where(lane == ids_ref[:, k : k + 1], gates_ref[:, k : k + 1], dense)
 
-    for source in peers:
-        where = (source, e)
-        arrive(got_stat.at[source], stat_send.at[source], stat_recv.at[source], where)
+    for k in range(N_CTX - 1):
+        arrive(got_stat.at[k], stat_send.at[k], stat_recv.at[k], (peers[k], e))
     stats = got_stat[...].reshape(N_CTX * 8, 128).T
     peak = top
     for source in range(N_CTX):
@@ -346,9 +346,11 @@
     for source in range(N_CTX):
         factor = jnp.exp(stats[:, 8 * source : 8 * source + 1] - peak)
         total = total + stats[:, 8 * source + 1 : 8 * source + 2] * factor
-    for source in peers:
-        arrive(got.at[source], part_send.at[source], part_recv.at[source], (source, e))
-    for source in range(N_CTX):
+    for source in (N_CTX - 1, *range(N_CTX - 1)):
+        if source < N_CTX - 1:
+            arrive(
+                got.at[source], part_send.at[source], part_recv.at[source], (peers[source], e)
+            )
         factor = jnp.exp(stats[:, 8 * source : 8 * source + 1] - peak)
         summed = summed + got[source].astype(F32) * factor
     attended = (summed / total).astype(BF16)

time: 121 us -> 119 us (0.983)
  Pallas kernels: 119 us -> 117 us
    pallas_call x1, Pallas kernels: 119 us -> 117 us  [per_device(): pl.pallas_call(layer_kernel, out_shape=jax.ShapeDtypeStruct((ROWS, COLS),...]
where the time goes in v6:
time: 119 us
  Pallas kernels  117 us (98%)
  local copies, waits for them, and re-layouts  1.36 us (1%)
    pallas_call x1, Pallas kernels, per_device(): pl.pallas_call(layer_kernel, out_shape=jax.ShapeDtypeStruct((ROWS, COLS),...  117 us

profile of v6, /device:TPU:1, one launch (start us, length us, event | category | flops | bytes accessed | tf_op | source)
XLA Modules:
  0.0 119.2 jit_solution(5475247613193396873)
XLA Ops:
  0.7 117.2 %layer.1 = bf16[16,896]{1,0:T(8,128)(2,1)} custom-call(s32[1]{0:T(128)S(6)} %copy.22.length_ref, s32[8]{0:T(128)} %bitcast.25, bf16[8,128,576]{2,1,0:T(8,128)(2,1)} %bitcast.17, bf16[576,512]{1,0:T(8,128)(2,1)} %bitcast.18, bf16[16,576]{1,0:T(8,128)(2,1)} %bitcast.22, s32[16,8]{1,0:T(8,128)} %bitcast.23, f32[16,8]{1,0:T(8,128)} %bitcast.24, ...), custom_call_target="tpu_custom_call" | custom-call | tf_op jit(solution)/shard_map/layer/pallas_call | solution.py:944
  117.9 1.4 %copy.23 = bf16[2,8,896]{2,1,0:T(8,128)(2,1)} copy(bf16[2,8,896]{2,1,0:T(8,128)(2,1)} %bitcast.20) | data formatting | bytes 57344

commit v7 on v6

--- a/solution.py
+++ b/solution.py
@@ -104,6 +104,9 @@
     shares,
     from_y,
     from_z,
+    ahead_z,
+    summed_z,
+    crossed_z,
     squares,
     state,
     notes,
@@ -137,6 +140,10 @@
     y_recv,
     zsum_send,
     zsum_recv,
+    ahead_send,
+    ahead_recv,
+    cross_z_send,
+    cross_z_recv,
     square_send,
     square_recv,
     note_send,
@@ -394,6 +401,7 @@
     fetches[0].wait()
     arrive(wo_other, pair_send.at[0], pair_recv.at[0], other_core)
     other_y = device(x, plus(y, 2), z, core)
+    y_first, z_first = pl.ds(0, 512), pl.ds(512, COLS - 512)
     for half in (1, 0):
         at = lax.rem(y_hi + half, 2)
         near_rows = pl.ds(pl.multiple_of(at * 128, 128), 128)
@@ -405,32 +413,63 @@
         if half:
             for step in (4, 3, 5, 2, 6, 1, 7, 0):
                 to = lax.rem(z + step, 8)
-                send(shares.at[at, to], from_y.at[to], y_send.at[to], y_recv.at[to], other_y)
+                send(
+                    shares.at[at, to, :, y_first],
+                    from_y.at[to, :, y_first],
+                    y_send.at[to],
+                    y_recv.at[to],
+                    other_y,
+                )
+    for step in (4, 3, 5, 2, 6, 1, 7):
+        to = lax.rem(z + step, 8)
+        send(
+            shares.at[:, to, :, z_first],
+            ahead_z.at[z],
+            ahead_send.at[to],
+            ahead_recv.at[z],
+            device(x, y, to, core),
+        )
     for step in (4, 3, 5, 2, 6, 1, 7, 0):
         to = lax.rem(z + step, 8)
-        arrive(from_y.at[to], y_send.at[to], y_recv.at[to], other_y)
-        both_y = shares[y_hi, to].astype(F32) + from_y[to].astype(F32)
+        arrive(from_y.at[to, :, y_first], y_send.at[to], y_recv.at[to], other_y)
+        both_y = shares[y_hi, to, :, y_first].astype(F32) + from_y[to, :, y_first].astype(F32)
         if step:
-            shares[y_hi, to] = both_y.astype(BF16)
+            shares[y_hi, to, :, y_first] = both_y.astype(BF16)
             send(
-                shares.at[y_hi, to],
-                from_z.at[z],
+                shares.at[y_hi, to, :, y_first],
+                from_z.at[z, :, y_first],
                 zsum_send.at[to],
                 zsum_recv.at[z],
                 device(x, y, to, core),
             )
-    fetches[5].wait()
-    value = residual_ref[...].astype(F32) + both_y
+    both_z = shares[:, z, :, z_first].astype(F32)
     for step in range(1, 8):
         source = lax.rem(z + step, 8)
         arrive(
-            from_z.at[source],
+            ahead_z.at[source],
+            ahead_send.at[source],
+            ahead_recv.at[source],
+            device(x, y, source, core),
+        )
+        both_z = both_z + ahead_z[source].astype(F32)
+    summed_z[...] = both_z.astype(BF16)
+    send(summed_z.at[1 - y_hi], crossed_z, cross_z_send, cross_z_recv, other_y)
+    fetches[5].wait()
+    value = residual_ref[:, y_first].astype(F32) + both_y
+    for step in range(1, 8):
+        source = lax.rem(z + step, 8)
+        arrive(
+            from_z.at[source, :, y_first],
             zsum_send.at[source],
             zsum_recv.at[source],
             device(x, y, source, core),
         )
-        value = value + from_z[source].astype(F32)
-    state[...] = value
+        value = value + from_z[source, :, y_first].astype(F32)
+    state[:, y_first] = value
+    arrive(crossed_z, cross_z_send, cross_z_recv, other_y)
+    value = residual_ref[:, z_first].astype(F32) + summed_z[y_hi].astype(F32)
+    state[:, z_first] = value + crossed_z[...].astype(F32)
+    value = state[...]
     rows[c, core, y_hi, z] = (value * gain_ref[:, columns]).astype(BF16)
     squares[c] = jnp.broadcast_to(jnp.sum(value * value, axis=-1, keepdims=True), (ROWS, 128))
     for target in peers:
@@ -867,13 +906,13 @@
     ring_sum(3)
     near_add(1)
     ring_sum(2)
+    wide_add(0, 2)
+    ring_sum(1)
     drain(earlier)
     all_heads.wait_send()
     all_notes.wait_send()
     for copy in shared:
         copy.wait_send()
-    wide_add(0, 2)
-    ring_sum(1)
     wide_add(1, 2)
     for step in (1, 3, 0):
         for part in range(2):
@@ -938,7 +977,7 @@
     expert_down,
 ):
     key_width = queries.shape[3]
-    pairs = [(N_CTX,), (N_CTX,), None, (N_CTX,), None, (8,), (8,), (N_CTX,), None]
+    pairs = [(N_CTX,), (N_CTX,), None, (N_CTX,), None, (8,), (8,), (8,), None, (N_CTX,), None]
     pairs += [(8,), (16,), (2, 3), (2, 2, 4), (2, 4), (2, 4, 4), (3,)]
     pairs += [(2,), None, (2, 2, 2), (2, 2, 4), (2, 3), (2, 4, 4), (16,), (2, 8)]
     out = pl.pallas_call(
@@ -966,6 +1005,9 @@
             pltpu.VMEM((2, 8, ROWS, COLS), BF16),
             pltpu.VMEM((8, ROWS, COLS), BF16),
             pltpu.VMEM((8, ROWS, COLS), BF16),
+            pltpu.VMEM((8, 2, ROWS, COLS - 512), BF16),
+            pltpu.VMEM((2, ROWS, COLS - 512), BF16),
+            pltpu.VMEM((ROWS, COLS - 512), BF16),
             pltpu.VMEM((N_CTX, ROWS, 128), F32),
             pltpu.VMEM((ROWS, COLS), F32),
             pltpu.VMEM((N_EXP, 1, 128), F32),

time: 119 us -> 119 us (level)
  no operation moved by 1% of the time
where the time goes in v7:
time: 119 us; the launch traced here: 118 us
  Pallas kernels  116 us (97%)
  local copies, waits for them, and re-layouts  1.36 us (1%)
    pallas_call x1, Pallas kernels, per_device(): pl.pallas_call(layer_kernel, out_shape=jax.ShapeDtypeStruct((ROWS, COLS),...  116 us

profile of v7, /device:TPU:1, one launch (start us, length us, event | category | flops | bytes accessed | tf_op | source)
XLA Modules:
  0.0 118.4 jit_solution(18230841096298571494)
XLA Ops:
  0.7 116.3 %layer.1 = bf16[16,896]{1,0:T(8,128)(2,1)} custom-call(s32[1]{0:T(128)S(6)} %copy.22.length_ref, s32[8]{0:T(128)} %bitcast.25, bf16[8,128,576]{2,1,0:T(8,128)(2,1)} %bitcast.17, bf16[576,512]{1,0:T(8,128)(2,1)} %bitcast.18, bf16[16,576]{1,0:T(8,128)(2,1)} %bitcast.22, s32[16,8]{1,0:T(8,128)} %bitcast.23, f32[16,8]{1,0:T(8,128)} %bitcast.24, ...), custom_call_target="tpu_custom_call" | custom-call | tf_op jit(solution)/shard_map/layer/pallas_call | solution.py:983
  117.0 1.4 %copy.23 = bf16[2,8,896]{2,1,0:T(8,128)(2,1)} copy(bf16[2,8,896]{2,1,0:T(8,128)(2,1)} %bitcast.20) | data formatting | bytes 57344
